TPU v7x, 32 devices: a whole 2x2x4 slice. The times are simulated.
32 devices in a mesh: leaf: 2 (over y), tok: 16 (over z, x, core).
Axes of the slice: x: 2, y: 2, z: 4, core: 2. Of those that a mesh axis runs over, the one named last changes fastest.
Arguments:
- hidden_in: bfloat16 [4, 2048, 1024], P('leaf', 'tok'), may hold values from -7 to 7
- output_cotangent: bfloat16 [4, 2048, 1024], P('leaf', 'tok'), may hold values from -6 to 6
- unit_place: int32 [4, 16], P('leaf'), may hold values from 0 to 15, as said below
- ln1_gain: bfloat16 [1024], P(('leaf', 'tok')), may hold values from 0.25 to 1.75
- ln1_bias: bfloat16 [1024], P(('leaf', 'tok')), may hold values from -1.5 to 1.5
- qkv_weight: bfloat16 [1024, 3072], P(('leaf', 'tok')), may hold values from -0.12617187 to 0.12617187
- qv_bias: bfloat16 [2048], P(('leaf', 'tok')), may hold values from -1.5 to 1.5
- out_weight: bfloat16 [1024, 1024], P(('leaf', 'tok')), may hold values from -0.5 to 0.5
- out_bias: bfloat16 [1024], P(('leaf', 'tok')), may hold values from -1.5 to 1.5
- ln2_gain: bfloat16 [1024], P(('leaf', 'tok')), may hold values from 0.25 to 1.75
- ln2_bias: bfloat16 [1024], P(('leaf', 'tok')), may hold values from -1.5 to 1.5
- fc1_weight: bfloat16 [1024, 4096], P(('leaf', 'tok')), may hold values from -0.1875 to 0.1875
- fc1_bias: bfloat16 [4096], P(('leaf', 'tok')), may hold values from -1.5 to 1.5
- fc2_weight: bfloat16 [4096, 1024], P(('leaf', 'tok')), may hold values from -0.09375 to 0.09375
- fc2_bias: bfloat16 [1024], P(('leaf', 'tok')), may hold values from -1.5 to 1.5
Outputs:
- layer_out: bfloat16 [4, 2048, 1024], P('leaf', 'tok')
- input_grad: bfloat16 [4, 2048, 1024], P('leaf', 'tok')
- ln1_gain_grad: float32 [1024], P(('leaf', 'tok'))
- ln1_bias_grad: float32 [1024], P(('leaf', 'tok'))
- qkv_weight_grad: float32 [1024, 3072], P(('leaf', 'tok'))
- qv_bias_grad: float32 [2048], P(('leaf', 'tok'))
- out_weight_grad: float32 [1024, 1024], P(('leaf', 'tok'))
- out_bias_grad: float32 [1024], P(('leaf', 'tok'))
- ln2_gain_grad: float32 [1024], P(('leaf', 'tok'))
- ln2_bias_grad: float32 [1024], P(('leaf', 'tok'))
- fc1_weight_grad: float32 [1024, 4096], P(('leaf', 'tok'))
- fc1_bias_grad: float32 [4096], P(('leaf', 'tok'))
- fc2_weight_grad: float32 [4096, 1024], P(('leaf', 'tok'))
- fc2_bias_grad: float32 [1024], P(('leaf', 'tok'))
Inputs may be any that keep to these rules, and one draw needn't show every extreme that they name: `unit_place`: each row is a permutation of 0 to 15. Units 0 to 3 are the trunk's quarters in order, 4 to 7 the branches, 8 to 15 the leaves; leaf 8 + k hangs from branch 4 + k // 2.
All inputs are finite; a program needn't handle non-finite values.
Results may differ from a plain program's by a relative error of at most 0.0085.
Values may be sent and summed in bfloat16 or wider, within the bound.
No kernel may reach another device: no remote copies, remote signals or barrier semaphores. Data moves between devices by JAX's collectives and lax.ppermute only.
A program may use at most 192 MiB of HBM per device.

v0:
```python
import jax
import jax.numpy as jnp
from jax import lax
from jax.sharding import PartitionSpec as P

HEADS = 16
UNITS = 16


layer_eps = 1e-05
masked_score = -1e30


def layer_norm(values, gain_vec, shift_vec):
    row_mean = jnp.mean(values, axis=-1, keepdims=True)
    centered = values - row_mean
    spread = jnp.mean(centered * centered, axis=-1, keepdims=True)
    return centered * lax.rsqrt(spread + layer_eps) * gain_vec + shift_vec


def gelu_tanh(values):
    return jax.nn.gelu(values, approximate=True)


def tree_layout(placement, tree_tokens):
    unit_len = tree_tokens // UNITS
    position = jnp.arange(tree_tokens, dtype=jnp.int32)
    slot_index = position // unit_len
    within = position - slot_index * unit_len
    picked = slot_index[None, :, None] == jnp.arange(UNITS, dtype=jnp.int32)[None, None, :]
    chosen = jnp.sum(jnp.where(picked, placement[:, None, :], 0), axis=2)
    offset = jnp.where(
        chosen < 4, chosen * unit_len, jnp.where(chosen < 8, 4 * unit_len, 5 * unit_len)
    )
    branches = jnp.where(chosen < 4, -1, jnp.where(chosen < 8, chosen - 4, (chosen - 8) // 2))
    leaves = jnp.where(chosen < 8, -1, chosen - 8)
    return (offset + within[None, :], branches, leaves)


def allowed_pairs(query_info, key_info):
    query_depth, query_branch, query_leaf = query_info
    key_depth, key_branch, key_leaf = key_info
    same_branch = (key_branch[:, None, :] < 0) | (
        key_branch[:, None, :] == query_branch[:, :, None]
    )
    same_leaf = (key_leaf[:, None, :] < 0) | (key_leaf[:, None, :] == query_leaf[:, :, None])
    earlier = key_depth[:, None, :] <= query_depth[:, :, None]
    distance = (query_depth[:, :, None] - key_depth[:, None, :]).astype(jnp.float32)
    return (same_branch & same_leaf & earlier, distance)


def pair_scores(query_heads, key_heads, query_info, key_info, head_slopes, score_scale):
    allowed, distance = allowed_pairs(query_info, key_info)
    raw_scores = (
        jnp.einsum("mrhe,mkhe->mhrk", query_heads, key_heads, preferred_element_type=jnp.float32)
        * score_scale
    )
    scores = raw_scores - head_slopes[None, :, None, None] * distance[:, None, :, :]
    scores = jnp.where(allowed[:, None, :, :], scores, masked_score)
    return (allowed, scores)


def block_terms(
    query_heads, gathered, query_info, key_info, head_slopes, score_scale, block_start, block_size
):
    micro_count, row_count, head_count, head_size = query_heads.shape
    model_width = head_count * head_size
    block_piece = lax.dynamic_slice_in_dim(gathered, block_start, block_size, 1)
    key_heads = block_piece[:, :, :model_width].reshape(
        micro_count, block_size, head_count, head_size
    )
    value_heads = block_piece[:, :, model_width:].reshape(
        micro_count, block_size, head_count, head_size
    )
    key_part = tuple(
        (lax.dynamic_slice_in_dim(layout, block_start, block_size, 1) for layout in key_info)
    )
    allowed, scores = pair_scores(
        query_heads, key_heads, query_info, key_part, head_slopes, score_scale
    )
    return (key_heads, value_heads, allowed, scores)


def attend_forward(
    query_heads, gathered, query_info, key_info, head_slopes, score_scale, block_size
):
    micro_count, row_count, head_count, head_size = query_heads.shape
    block_count = gathered.shape[1] // block_size

    def first_pass(block_index, state_pair):
        running_max, running_sum = state_pair
        unused_keys, unused_values, allowed, scores = block_terms(
            query_heads,
            gathered,
            query_info,
            key_info,
            head_slopes,
            score_scale,
            block_index * block_size,
            block_size,
        )
        new_max = jnp.maximum(running_max, jnp.max(scores, axis=-1))
        weights = jnp.where(allowed[:, None, :, :], jnp.exp(scores - new_max[..., None]), 0.0)
        return (new_max, running_sum * jnp.exp(running_max - new_max) + jnp.sum(weights, axis=-1))

    start_max = jnp.full((micro_count, head_count, row_count), masked_score, jnp.float32)
    running_max, running_sum = lax.fori_loop(
        0, block_count, first_pass, (start_max, jnp.zeros_like(start_max))
    )
    log_total = running_max + jnp.log(running_sum)

    def second_pass(block_index, context):
        unused_keys, value_heads, allowed, scores = block_terms(
            query_heads,
            gathered,
            query_info,
            key_info,
            head_slopes,
            score_scale,
            block_index * block_size,
            block_size,
        )
        probs = jnp.where(
            allowed[:, None, :, :], jnp.exp(scores - log_total[..., None]), 0.0
        ).astype(jnp.bfloat16)
        return context + jnp.einsum(
            "mhrk,mkhe->mrhe", probs, value_heads, preferred_element_type=jnp.float32
        )

    context = lax.fori_loop(
        0,
        block_count,
        second_pass,
        jnp.zeros((micro_count, row_count, head_count, head_size), jnp.float32),
    )
    return (context, log_total)


def attend_backward(
    query_heads,
    gathered,
    query_info,
    key_info,
    head_slopes,
    score_scale,
    block_size,
    log_total,
    grad_context,
):
    micro_count, row_count, head_count, head_size = query_heads.shape
    model_width = head_count * head_size
    block_count = gathered.shape[1] // block_size

    def probs_of(block_index):
        key_heads, value_heads, allowed, scores = block_terms(
            query_heads,
            gathered,
            query_info,
            key_info,
            head_slopes,
            score_scale,
            block_index * block_size,
            block_size,
        )
        probs = jnp.where(allowed[:, None, :, :], jnp.exp(scores - log_total[..., None]), 0.0)
        grad_probs = jnp.einsum(
            "mrhe,mkhe->mhrk", grad_context, value_heads, preferred_element_type=jnp.float32
        )
        return (key_heads, probs, grad_probs)

    def delta_pass(block_index, row_delta):
        unused_keys, probs, grad_probs = probs_of(block_index)
        return row_delta + jnp.sum(probs * grad_probs, axis=-1)

    row_delta = lax.fori_loop(0, block_count, delta_pass, jnp.zeros_like(log_total))

    def grad_pass(block_index, state_pair):
        grad_query, key_grads = state_pair
        key_heads, probs, grad_probs = probs_of(block_index)
        grad_scores = (probs * (grad_probs - row_delta[..., None])).astype(jnp.bfloat16)
        grad_query = (
            grad_query
            + jnp.einsum(
                "mhrk,mkhe->mrhe", grad_scores, key_heads, preferred_element_type=jnp.float32
            )
            * score_scale
        )
        grad_keys = (
            jnp.einsum(
                "mhrk,mrhe->mkhe", grad_scores, query_heads, preferred_element_type=jnp.float32
            )
            * score_scale
        )
        grad_values = jnp.einsum(
            "mhrk,mrhe->mkhe",
            probs.astype(jnp.bfloat16),
            grad_context,
            preferred_element_type=jnp.float32,
        )
        block_piece = jnp.concatenate(
            [
                grad_keys.reshape(micro_count, block_size, model_width),
                grad_values.reshape(micro_count, block_size, model_width),
            ],
            axis=2,
        )
        key_grads = lax.dynamic_update_slice_in_dim(
            key_grads, block_piece, block_index * block_size, 1
        )
        return (grad_query, key_grads)

    start_query = jnp.zeros((micro_count, row_count, head_count, head_size), jnp.float32)
    start_keys = jnp.zeros((micro_count, gathered.shape[1], 2 * model_width), jnp.float32)
    grad_query, key_grads = lax.fori_loop(0, block_count, grad_pass, (start_query, start_keys))
    return (grad_query, key_grads, row_delta)


def on_device(
    hidden_in,
    output_cotangent,
    unit_place,
    ln1_gain,
    ln1_bias,
    qkv_weight,
    qv_bias,
    out_weight,
    out_bias,
    ln2_gain,
    ln2_bias,
    fc1_weight,
    fc1_bias,
    fc2_weight,
    fc2_bias,
):
    micro_count, row_count, model_width = hidden_in.shape
    head_count = HEADS
    head_size = model_width // head_count
    score_scale = head_size ** (-0.5)
    tree_tokens = row_count * lax.axis_size("tok")
    block_size = min(512, tree_tokens)
    head_slopes = jnp.power(
        2.0, -8.0 * (jnp.arange(head_count, dtype=jnp.float32) + 1.0) / head_count
    )
    key_info = tree_layout(unit_place, tree_tokens)
    own_start = lax.axis_index("tok") * row_count
    query_info = tuple(
        (lax.dynamic_slice_in_dim(layout, own_start, row_count, 1) for layout in key_info)
    )
    (
        gain_one,
        shift_one,
        w_mixed,
        bias_mixed,
        w_output,
        bias_output,
        gain_two,
        shift_two,
        up_weight,
        bias_expand,
        down_weight,
        bias_reduce,
    ) = (
        lax.all_gather(ln1_gain, ("leaf", "tok"), axis=0, tiled=True),
        lax.all_gather(ln1_bias, ("leaf", "tok"), axis=0, tiled=True),
        lax.all_gather(qkv_weight, ("leaf", "tok"), axis=0, tiled=True),
        lax.all_gather(qv_bias, ("leaf", "tok"), axis=0, tiled=True),
        lax.all_gather(out_weight, ("leaf", "tok"), axis=0, tiled=True),
        lax.all_gather(out_bias, ("leaf", "tok"), axis=0, tiled=True),
        lax.all_gather(ln2_gain, ("leaf", "tok"), axis=0, tiled=True),
        lax.all_gather(ln2_bias, ("leaf", "tok"), axis=0, tiled=True),
        lax.all_gather(fc1_weight, ("leaf", "tok"), axis=0, tiled=True),
        lax.all_gather(fc1_bias, ("leaf", "tok"), axis=0, tiled=True),
        lax.all_gather(fc2_weight, ("leaf", "tok"), axis=0, tiled=True),
        lax.all_gather(fc2_bias, ("leaf", "tok"), axis=0, tiled=True),
    )
    hidden = hidden_in.astype(jnp.float32)
    normed_one = layer_norm(
        hidden, gain_one.astype(jnp.float32), shift_one.astype(jnp.float32)
    ).astype(jnp.bfloat16)
    projected = jnp.einsum("mrd,de->mre", normed_one, w_mixed, preferred_element_type=jnp.float32)
    mixed_bias = bias_mixed.astype(jnp.float32)
    queries = (projected[..., :model_width] + mixed_bias[:model_width]).astype(jnp.bfloat16)
    key_rows = projected[..., model_width : 2 * model_width].astype(jnp.bfloat16)
    values = (projected[..., 2 * model_width :] + mixed_bias[model_width:]).astype(jnp.bfloat16)
    own_pairs = jnp.concatenate([key_rows, values], axis=2)
    gathered = lax.all_gather(own_pairs, "tok", axis=1, tiled=True)
    query_heads = queries.reshape(micro_count, row_count, head_count, head_size)
    context, log_total = attend_forward(
        query_heads, gathered, query_info, key_info, head_slopes, score_scale, block_size
    )
    context = context.reshape(micro_count, row_count, model_width).astype(jnp.bfloat16)
    branch_out = jnp.einsum(
        "mrd,de->mre", context, w_output, preferred_element_type=jnp.float32
    ) + bias_output.astype(jnp.float32)
    middle = hidden + branch_out
    second_normalized = layer_norm(
        middle, gain_two.astype(jnp.float32), shift_two.astype(jnp.float32)
    ).astype(jnp.bfloat16)
    expand = jnp.einsum(
        "lyh,ha->lya", second_normalized, up_weight, preferred_element_type=jnp.float32
    ) + bias_expand.astype(jnp.float32)
    activated_hidden = gelu_tanh(expand).astype(jnp.bfloat16)
    reduced = jnp.einsum(
        "thy,yq->thq", activated_hidden, down_weight, preferred_element_type=jnp.float32
    ) + bias_reduce.astype(jnp.float32)
    layer_out = (middle + reduced).astype(jnp.bfloat16)
    (
        gain_one,
        shift_one,
        w_mixed,
        bias_mixed,
        w_output,
        bias_output,
        gain_two,
        shift_two,
        up_weight,
        bias_expand,
        down_weight,
        bias_reduce,
    ) = (
        lax.all_gather(ln1_gain, ("leaf", "tok"), axis=0, tiled=True),
        lax.all_gather(ln1_bias, ("leaf", "tok"), axis=0, tiled=True),
        lax.all_gather(qkv_weight, ("leaf", "tok"), axis=0, tiled=True),
        lax.all_gather(qv_bias, ("leaf", "tok"), axis=0, tiled=True),
        lax.all_gather(out_weight, ("leaf", "tok"), axis=0, tiled=True),
        lax.all_gather(out_bias, ("leaf", "tok"), axis=0, tiled=True),
        lax.all_gather(ln2_gain, ("leaf", "tok"), axis=0, tiled=True),
        lax.all_gather(ln2_bias, ("leaf", "tok"), axis=0, tiled=True),
        lax.all_gather(fc1_weight, ("leaf", "tok"), axis=0, tiled=True),
        lax.all_gather(fc1_bias, ("leaf", "tok"), axis=0, tiled=True),
        lax.all_gather(fc2_weight, ("leaf", "tok"), axis=0, tiled=True),
        lax.all_gather(fc2_bias, ("leaf", "tok"), axis=0, tiled=True),
    )
    grad_out = output_cotangent.astype(jnp.float32)
    down_weight_gradient = jnp.einsum(
        "wlt,wlc->tc", activated_hidden, output_cotangent, preferred_element_type=jnp.float32
    )
    g_b_reduce = jnp.sum(grad_out, axis=(0, 1))
    activated_gradient = jnp.einsum(
        "yec,oc->yeo", output_cotangent, down_weight, preferred_element_type=jnp.float32
    )
    ignored, gelu_back = jax.vjp(gelu_tanh, expand)
    up_projection_gradient = gelu_back(activated_gradient)[0].astype(jnp.bfloat16)
    g_b_expand = jnp.sum(up_projection_gradient, axis=(0, 1), dtype=jnp.float32)
    g_w_expand = jnp.einsum(
        "vsl,vsi->li", second_normalized, up_projection_gradient, preferred_element_type=jnp.float32
    )
    grad_normed_two = jnp.einsum(
        "xgt,st->xgs", up_projection_gradient, up_weight, preferred_element_type=jnp.float32
    )
    ignored, second_back = jax.vjp(
        layer_norm, middle, gain_two.astype(jnp.float32), shift_two.astype(jnp.float32)
    )
    grad_middle_part, g_gain_two, g_shift_two = second_back(grad_normed_two)
    grad_middle = grad_out + grad_middle_part
    grad_branch = grad_middle.astype(jnp.bfloat16)
    g_b_output = jnp.sum(grad_branch, axis=(0, 1), dtype=jnp.float32)
    g_w_output = jnp.einsum("mrd,mre->de", context, grad_branch, preferred_element_type=jnp.float32)
    grad_context = jnp.einsum(
        "mre,de->mrd", grad_branch, w_output, preferred_element_type=jnp.float32
    ).astype(jnp.bfloat16)
    gathered = lax.all_gather(own_pairs, "tok", axis=1, tiled=True)
    context_heads = grad_context.reshape(micro_count, row_count, head_count, head_size)
    grad_query, key_grads, row_delta = attend_backward(
        query_heads,
        gathered,
        query_info,
        key_info,
        head_slopes,
        score_scale,
        block_size,
        log_total,
        context_heads,
    )
    own_key_grads = lax.psum_scatter(
        key_grads.astype(jnp.bfloat16), "tok", scatter_dimension=1, tiled=True
    )
    grad_queries = grad_query.reshape(micro_count, row_count, model_width).astype(jnp.bfloat16)
    grad_projected = jnp.concatenate([grad_queries, own_key_grads], axis=2)
    g_b_mixed = jnp.concatenate(
        [
            jnp.sum(grad_queries, axis=(0, 1), dtype=jnp.float32),
            jnp.sum(own_key_grads[..., model_width:], axis=(0, 1), dtype=jnp.float32),
        ]
    )
    g_w_mixed = jnp.einsum(
        "mrd,mre->de", normed_one, grad_projected, preferred_element_type=jnp.float32
    )
    grad_normed_one = jnp.einsum(
        "mre,de->mrd", grad_projected, w_mixed, preferred_element_type=jnp.float32
    )
    ignored, first_back = jax.vjp(
        layer_norm, hidden, gain_one.astype(jnp.float32), shift_one.astype(jnp.float32)
    )
    grad_hidden_part, g_gain_one, g_shift_one = first_back(grad_normed_one)
    input_grad = (grad_middle + grad_hidden_part).astype(jnp.bfloat16)
    owned = (
        lax.psum_scatter(g_gain_one, ("leaf", "tok"), scatter_dimension=0, tiled=True),
        lax.psum_scatter(g_shift_one, ("leaf", "tok"), scatter_dimension=0, tiled=True),
        lax.psum_scatter(g_w_mixed, ("leaf", "tok"), scatter_dimension=0, tiled=True),
        lax.psum_scatter(g_b_mixed, ("leaf", "tok"), scatter_dimension=0, tiled=True),
        lax.psum_scatter(g_w_output, ("leaf", "tok"), scatter_dimension=0, tiled=True),
        lax.psum_scatter(g_b_output, ("leaf", "tok"), scatter_dimension=0, tiled=True),
        lax.psum_scatter(g_gain_two, ("leaf", "tok"), scatter_dimension=0, tiled=True),
        lax.psum_scatter(g_shift_two, ("leaf", "tok"), scatter_dimension=0, tiled=True),
        lax.psum_scatter(g_w_expand, ("leaf", "tok"), scatter_dimension=0, tiled=True),
        lax.psum_scatter(g_b_expand, ("leaf", "tok"), scatter_dimension=0, tiled=True),
        lax.psum_scatter(down_weight_gradient, ("leaf", "tok"), scatter_dimension=0, tiled=True),
        lax.psum_scatter(g_b_reduce, ("leaf", "tok"), scatter_dimension=0, tiled=True),
    )
    return (layer_out, input_grad) + tuple(owned)


def solution(mesh):
    return jax.shard_map(
        on_device,
        mesh=mesh,
        in_specs=(
            P("leaf", "tok", None),
            P("leaf", "tok", None),
            P("leaf", None),
            P(("leaf", "tok")),
            P(("leaf", "tok")),
            P(("leaf", "tok"), None),
            P(("leaf", "tok")),
            P(("leaf", "tok"), None),
            P(("leaf", "tok")),
            P(("leaf", "tok")),
            P(("leaf", "tok")),
            P(("leaf", "tok"), None),
            P(("leaf", "tok")),
            P(("leaf", "tok"), None),
            P(("leaf", "tok")),
        ),
        out_specs=(
            P("leaf", "tok", None),
            P("leaf", "tok", None),
            P(("leaf", "tok")),
            P(("leaf", "tok")),
            P(("leaf", "tok"), None),
            P(("leaf", "tok")),
            P(("leaf", "tok"), None),
            P(("leaf", "tok")),
            P(("leaf", "tok")),
            P(("leaf", "tok")),
            P(("leaf", "tok"), None),
            P(("leaf", "tok")),
            P(("leaf", "tok"), None),
            P(("leaf", "tok")),
        ),
        check_vma=False,
    )
```

profile of v0, /device:TPU:0, one launch (start us, length us, event | category | flops | bytes accessed | tf_op | source)
XLA Modules:
  0.0 1473.3 jit_solution(3086529884863443979)
XLA Ops:
  13.8 42.4 %all-reduce.16 = (bf16[1024]{0:T(1024)(128)(2,1)S(1)}, bf16[1024]{0:T(1024)(128)(2,1)S(1)}, bf16[2048]{0:T(1024)(128)(2,1)S(1)}, bf16[1024]{0:T(1024)(128)(2,1)S...) all-reduce(bf16[1024]{0:T(1024)(128)(2,1)S(1)} %dynamic-update-slic, ...), channel_id=1, replica_groups=mesh['leaf'=2,'tok'=16] {'leaf','tok'}, use_global_device_ids=true, to_apply=%add.1 | all-reduce | flops 8192 | bytes 32768
  59.4 23.8 %all-gather.7.cloned.1.call-done = bf16[1024,3072]{1,0:T(8,128)(2,1)} async-done(((bf16[32,3072]{1,0:T(8,128)(2,1)}), bf16[1024,3072]{1,0:T(8,128)(2,1)}) %all-gather.7.cloned.1.call-update) | async-done | bytes 6291472 | tf_op jit(solution)/shard_map/all_gather | solution.py:265
  83.2 4.9 fusion.58
  91.6 39.7 %all-gather = bf16[32,1,128]{2,1,0:T(2,128)(2,1)S(1)} all-gather(bf16[1,1,128]{2,1,0:T(2,128)(2,1)S(1)} %bitcast.255), channel_id=1, replica_groups=mesh['leaf'=2,'tok'=16] {'leaf','tok'}, dimensions={0}, use_global_device_ids=true | all-gather | bytes 8448 | tf_op jit(solution)/shard_map/all_gather | solution.py:272
  131.9 83.2 %all-gather.9.cloned.1.call-done = bf16[2,2048,2048]{2,1,0:T(8,128)(2,1)} async-done(((bf16[2,128,2048]{2,1,0:T(8,128)(2,1)}), bf16[2,2048,2048]{2,1,0:T(8,128)(2,1)}) %all-gather.9.cloned.1.call-update) | async-done | bytes 16777232 | tf_op jit(solution)/shard_map/all_gather | solution.py:286
  215.2 22.4 %copy.85 = bf16[2,2048,2048]{1,2,0:T(8,128)(2,1)} copy(bf16[2,2048,2048]{2,1,0:T(8,128)(2,1)} %all-gather.9.cloned.1.call-done) | data formatting | bytes 33554432
  237.6 33.7 %while.60 = (s32[]{:T(128)}, f32[2,16,128]{2,1,0:T(8,128)S(1)}, f32[2,16,128]{2,1,0:T(8,128)S(1)}, s32[2,2048]{1,0:T(2,128)S(1)}, s32[2,128]{1,0:T(2,128)S(1)}, ...) while((s32[]{:T(128)}, f32[2,16,128]{2,1,0:T(8,128)S(1)}, ...), condition=%wide.region_6.7_spmd.clone, body=%wide.region_3.6_spmd.clone.sunk | while | flops 294803488 | bytes 25821592 | solution.py:107
  240.7 2.6 fusion.181
  243.3 2.7 select_reduce_fusion.3
  249.1 2.6 fusion.181
  251.8 2.7 select_reduce_fusion.3
  257.6 2.6 fusion.181
  260.2 2.7 select_reduce_fusion.3
  266.0 2.6 fusion.181
  268.6 2.7 select_reduce_fusion.3
  271.4 51.6 %while.61 = (s32[]{:T(128)}, f32[2,128,16,64]{1,3,2,0:T(8,128)}, bf16[2,2048,2048]{1,2,0:T(8,128)(2,1)}, s32[2,2048]{1,0:T(2,128)S(1)}, s32[2,128]{1,0:T(2,128)S...) while((s32[]{:T(128)}, f32[2,128,16,64]{1,3,2,0:T(8,128)}, ...), condition=%wide.region_8.9_spmd.clone, body=%wide.region_7.8_spmd.clone.sunk | while | flops 553257024 | bytes 16580977 | solution.py:130
  273.5 4.0 constant_dynamic-slice_fusion.40
  277.5 6.5 fusion.187
  286.0 4.0 constant_dynamic-slice_fusion.40
  290.0 6.8 fusion.187
  298.9 4.2 constant_dynamic-slice_fusion.40
  303.1 6.8 fusion.187
  312.0 4.0 constant_dynamic-slice_fusion.40
  316.0 6.8 fusion.187
  327.2 24.6 %all-gather.13.cloned.1.call-done = bf16[1024,4096]{1,0:T(8,128)(2,1)} async-done(((bf16[32,4096]{1,0:T(8,128)(2,1)}), bf16[1024,4096]{1,0:T(8,128)(2,1)}) %all-gather.13.cloned.1.call-update) | async-done | bytes 8388624 | tf_op jit(solution)/shard_map/all_gather | solution.py:271
  351.7 7.9 fusion.60
  359.6 70.9 %all-gather.15.cloned.1.call-done = bf16[4096,1024]{1,0:T(8,128)(2,1)} async-done(((bf16[128,1024]{1,0:T(8,128)(2,1)}), bf16[4096,1024]{1,0:T(8,128)(2,1)}) %all-gather.15.cloned.1.call-update) | async-done | bytes 8388624 | tf_op jit(solution)/shard_map/all_gather | solution.py:273
  430.5 12.1 convert_reduce_fusion
  442.6 3.2 multiply_reduce_fusion
  449.1 39.6 %while.62 = (s32[]{:T(128)}, f32[2,16,128]{2,1,0:T(8,128)S(1)}, s32[2,2048]{1,0:T(2,128)S(1)}, s32[2,128]{1,0:T(2,128)S(1)}, s32[2,2048]{1,0:T(2,128)S(1)}, /*in...) while((s32[]{:T(128)}, f32[2,16,128]{2,1,0:T(8,128)S(1)}, ...), condition=%wide.region_15.16_spmd.clone, body=%wide.region_13.15_spmd.clone.sunk | while | flops 554833920 | bytes 31850872 | solution.py:175
  454.8 4.6 fusion.193
  464.6 4.6 fusion.193
  474.3 4.6 fusion.193
  484.1 4.6 fusion.193
  488.7 6.0 broadcast_in_dim.358.clone
  494.7 119.0 %while.63 = (s32[]{:T(128)}, f32[2,128,16,64]{1,3,2,0:T(8,128)S(1)}, bf16[2,2048,2048]{2,1,0:T(8,128)(2,1)}, bf16[2,2048,2048]{1,2,0:T(8,128)(2,1)}, s32[2,2048]...) while((s32[]{:T(128)}, ...), condition=%wide.region_17.18_spmd.clone, body=%wide.region_16.17_spmd.clone.sunk | while | flops 1388185600 | bytes 88048080 | solution.py:214
  499.9 4.7 fusion.205
  504.7 3.5 fusion.207
  513.5 6.3 copy.123
  519.7 4.8 constant_dynamic-update-slice_fusion.2
  529.7 4.7 fusion.205
  534.4 3.5 fusion.207
  543.2 6.3 copy.123
  549.5 4.8 constant_dynamic-update-slice_fusion.2
  559.5 4.7 fusion.205
  564.2 3.5 fusion.207
  573.0 6.3 copy.123
  579.3 4.8 constant_dynamic-update-slice_fusion.2
  589.2 4.7 fusion.205
  593.9 3.5 fusion.207
  602.8 6.3 copy.123
  609.0 4.7 constant_dynamic-update-slice_fusion.2
  615.0 2.8 convolution_bitcast_fusion.3
  618.0 14.1 convolution_bitcast_fusion
  633.5 10.5 convolution_bitcast_fusion.1
  646.2 144.9 %reduce-scatter.6.cloned.1.call-done = bf16[2,128,2048]{2,1,0:T(8,128)(2,1)} async-done(((bf16[2,2048,2048]{2,1,0:T(8,128)(2,1)}), bf16[2,128,2048]{2,1,0:T(8,128)(2,1)}) %reduce-scatter.6.cloned.1.call-update) | async-done | bytes 1048592 | tf_op jit(solution)/shard_map/reduce_scatter | solution.py:375
  791.1 7.7 convolution_bitcast_fusion.2
  799.5 8.3 fusion.91
  808.0 5.0 fusion.117
  815.0 40.5 %all-reduce.15 = (f32[1024]{0:T(1024)S(1)}, f32[1024]{0:T(1024)S(1)}, f32[2048]{0:T(1024)S(1)}, f32[1024]{0:T(1024)S(1)}, f32[1024]{0:T(1024)S(1)}, /*index=5*/f...) all-reduce(f32[1024]{0:T(1024)S(1)} %get-tuple-element.1236, ...), channel_id=3, replica_groups=mesh['leaf'=2,'tok'=16] {'leaf','tok'}, use_global_device_ids=true, to_apply=%region_22.23.clone | all-reduce | flops 12288 | bytes 98304
  860.1 74.3 %reduce-scatter.10.cloned.1.call-done = f32[32,1024]{1,0:T(8,128)} async-done(((f32[1024,1024]{1,0:T(8,128)}), f32[32,1024]{1,0:T(8,128)}) %reduce-scatter.10.cloned.1.call-update) | async-done | bytes 131088 | tf_op jit(solution)/shard_map/reduce_scatter | solution.py:402
  934.4 180.0 %reduce-scatter.14.cloned.1.call-done = f32[128,1024]{1,0:T(8,128)} async-done(((f32[4096,1024]{1,0:T(8,128)}), f32[128,1024]{1,0:T(8,128)}) %reduce-scatter.14.cloned.1.call-update) | async-done | bytes 524304 | tf_op jit(solution)/shard_map/reduce_scatter | solution.py:408
  1114.4 187.0 %reduce-scatter.12.cloned.1.call-done = f32[32,4096]{1,0:T(8,128)} async-done(((f32[1024,4096]{1,0:T(8,128)}), f32[32,4096]{1,0:T(8,128)}) %reduce-scatter.12.cloned.1.call-update) | async-done | bytes 524304 | tf_op jit(solution)/shard_map/reduce_scatter | solution.py:406
  1301.4 164.9 %reduce-scatter.8.cloned.1.call-done = f32[32,3072]{1,0:T(8,128)} async-done(((f32[1024,3072]{1,0:T(8,128)}), f32[32,3072]{1,0:T(8,128)}) %reduce-scatter.8.cloned.1.call-update) | async-done | bytes 393232 | tf_op jit(solution)/shard_map/reduce_scatter | solution.py:400
  (312 shorter events, 116.3 us)
Async XLA Ops:
  7.2 76.0 %all-gather.7.cloned.1.call-start = ((), (), s32[]{:S(2)}) async-start(), calls=%async_computation.5 | async-start | bytes 6488064 | tf_op jit(solution)/shard_map/all_gather | solution.py:265
  7.9 207.3 %all-gather.9.cloned.1.call-start = ((), (), s32[]{:S(2)}) async-start(), calls=%async_computation.6 | async-start | bytes 17825792 | tf_op jit(solution)/shard_map/all_gather | solution.py:286
  56.3 31.8 %copy-start.24 = (f32[1024]{0:T(1024)}, f32[1024]{0:T(1024)S(1)}, u32[]{:S(2)}) copy-start(f32[1024]{0:T(1024)S(1)} %convert_element_type.159) | copy-start | bytes 12292
  56.3 31.8 %copy-start.18 = (f32[1024]{0:T(1024)}, f32[1024]{0:T(1024)S(1)}, u32[]{:S(2)}) copy-start(f32[1024]{0:T(1024)S(1)} %convert_element_type.158) | copy-start | bytes 12292
  57.5 30.6 %copy-start.26 = (f32[2,128]{1,0:T(2,128)}, f32[2,128]{1,0:T(2,128)S(1)}, u32[]{:S(2)}) copy-start(f32[2,128]{1,0:T(2,128)S(1)} %broadcast_multiply_fusion.1) | copy-start | bytes 3076
  58.8 0.6 copy-start.38
  59.4 28.7 %copy-start.30 = (f32[2,128]{1,0:T(2,128)}, f32[2,128]{1,0:T(2,128)S(1)}, u32[]{:S(2)}) copy-start(f32[2,128]{1,0:T(2,128)S(1)} %fusion.113) | copy-start | bytes 3076
  88.1 3.5 copy-start.44
  88.1 43.3 %copy-start.43 = (s32[2,16]{1,0:T(2,128)S(1)}, s32[2,16]{1,0:T(2,128)}, u32[]{:S(2)}) copy-start(s32[2,16]{1,0:T(2,128)} %param.25) | copy-start | bytes 388
  89.5 234.8 %all-gather.11.cloned.1.call-start = ((), (), s32[]{:S(2)}) async-start(), calls=%async_computation.7 | async-start | bytes 2162688 | tf_op jit(solution)/shard_map/all_gather | solution.py:267
  90.3 261.5 %all-gather.13.cloned.1.call-start = ((), (), s32[]{:S(2)}) async-start(), calls=%async_computation.8 | async-start | bytes 8650752 | tf_op jit(solution)/shard_map/all_gather | solution.py:271
  90.9 339.7 %all-gather.15.cloned.1.call-start = ((), (), s32[]{:S(2)}) async-start(), calls=%async_computation.9 | async-start | bytes 8650752 | tf_op jit(solution)/shard_map/all_gather | solution.py:273
  91.4 699.6 %reduce-scatter.6.cloned.1.call-start = ((), (), s32[]{:S(2)}) async-start(), calls=%async_computation.10 | async-start | bytes 17825792 | tf_op jit(solution)/shard_map/reduce_scatter | solution.py:375
  91.6 354.2 %copy-start.20 = (f32[1024]{0:T(1024)}, f32[1024]{0:T(1024)S(1)}, u32[]{:S(2)}) copy-start(f32[1024]{0:T(1024)S(1)} %convert_element_type.167) | copy-start | bytes 12292
  91.6 260.1 %copy-start.22 = (f32[1024]{0:T(1024)}, f32[1024]{0:T(1024)S(1)}, u32[]{:S(2)}) copy-start(f32[1024]{0:T(1024)S(1)} %convert_element_type.168) | copy-start | bytes 12292
  271.4 52.9 %copy-start.1 = (bf16[2,128,1024]{2,1,0:T(8,128)(2,1)S(1)}, bf16[2,128,1024]{2,1,0:T(8,128)(2,1)}, u32[]{:S(2)}) copy-start(bf16[2,128,1024]{2,1,0:T(8,128)(2,1)} %param.23) | copy-start | bytes 1572868
  324.3 35.3 %copy-start.7 = (bf16[2,128,16,64]{1,3,2,0:T(8,128)(2,1)}, bf16[2,128,16,64]{1,3,2,0:T(8,128)(2,1)S(1)}, u32[]{:S(2)}) copy-start(bf16[2,128,16,64]{1,3,2,0:T(8,128)(2,1)S(1)} %convert_element_type.164) | copy-start | bytes 1572868
  326.9 118.9 %copy-start.3 = (f32[2,128,1024]{2,1,0:T(8,128)}, f32[2,128,1024]{2,1,0:T(8,128)S(1)}, u32[]{:S(2)}) copy-start(f32[2,128,1024]{2,1,0:T(8,128)S(1)} %get-tuple-element.1400) | copy-start | bytes 3145732
  326.9 118.9 %copy-start.28 = (f32[2,128]{1,0:T(2,128)}, f32[2,128]{1,0:T(2,128)S(1)}, u32[]{:S(2)}) copy-start(f32[2,128]{1,0:T(2,128)S(1)} %broadcast_multiply_fusion) | copy-start | bytes 3076
  327.2 118.7 %copy-start.32 = (f32[2,128]{1,0:T(2,128)}, f32[2,128]{1,0:T(2,128)S(1)}, u32[]{:S(2)}) copy-start(f32[2,128]{1,0:T(2,128)S(1)} %fusion.114) | copy-start | bytes 3076
  351.7 78.8 %copy-start.9 = (bf16[2,128,1024]{2,1,0:T(8,128)(2,1)S(1)}, bf16[2,128,1024]{2,1,0:T(8,128)(2,1)}, u32[]{:S(2)}) copy-start(bf16[2,128,1024]{2,1,0:T(8,128)(2,1)} %param.24) | copy-start | bytes 1572868
  430.5 12.1 copy-start.45
  442.6 3.2 copy-start.12
  445.8 2.3 copy-start.13
  446.2 1.0 copy-start.5
  446.3 2.9 copy-start.36
  448.1 1.0 copy-start.14
  488.7 6.0 copy-start
  613.8 1.0 copy-start.8
  613.8 1.2 copy-start.15
  613.8 4.2 copy-start.10
  613.8 320.6 %reduce-scatter.10.cloned.1.call-start = ((), (), s32[]{:S(2)}) async-start(), calls=%async_computation.12 | async-start | bytes 4325376 | tf_op jit(solution)/shard_map/reduce_scatter | solution.py:402
  617.8 496.6 %reduce-scatter.14.cloned.1.call-start = ((), (), s32[]{:S(2)}) async-start(), calls=%async_computation.14 | async-start | bytes 17301504 | tf_op jit(solution)/shard_map/reduce_scatter | solution.py:408
  632.1 1.4 copy-start.4
  632.1 1.4 copy-start.21
  632.1 1.4 copy-start.23
  632.1 1.4 copy-start.29
  632.1 1.4 copy-start.33
  632.1 669.2 %reduce-scatter.12.cloned.1.call-start = ((), (), s32[]{:S(2)}) async-start(), calls=%async_computation.13 | async-start | bytes 17301504 | tf_op jit(solution)/shard_map/reduce_scatter | solution.py:406
  644.0 147.1 %copy-start.2 = (bf16[2,128,1024]{2,1,0:T(8,128)(2,1)S(1)}, bf16[2,128,1024]{2,1,0:T(8,128)(2,1)}, u32[]{:S(2)}) copy-start(bf16[2,128,1024]{2,1,0:T(8,128)(2,1)} %param.23) | copy-start | bytes 1572868
  644.0 147.1 %copy-start.19 = (f32[1024]{0:T(1024)S(1)}, f32[1024]{0:T(1024)}, u32[]{:S(2)}) copy-start(f32[1024]{0:T(1024)} %copy-done.18) | copy-start | bytes 12292
  644.0 147.1 %copy-start.25 = (f32[1024]{0:T(1024)S(1)}, f32[1024]{0:T(1024)}, u32[]{:S(2)}) copy-start(f32[1024]{0:T(1024)} %copy-done.24) | copy-start | bytes 12292
  644.0 147.1 %copy-start.27 = (f32[2,128]{1,0:T(2,128)S(1)}, f32[2,128]{1,0:T(2,128)}, u32[]{:S(2)}) copy-start(f32[2,128]{1,0:T(2,128)} %copy-done.26) | copy-start | bytes 3076
  644.0 147.1 %copy-start.31 = (f32[2,128]{1,0:T(2,128)S(1)}, f32[2,128]{1,0:T(2,128)}, u32[]{:S(2)}) copy-start(f32[2,128]{1,0:T(2,128)} %copy-done.30) | copy-start | bytes 3076
  644.0 822.2 %reduce-scatter.8.cloned.1.call-start = ((), (), s32[]{:S(2)}) async-start(), calls=%async_computation.11 | async-start | bytes 12976128 | tf_op jit(solution)/shard_map/reduce_scatter | solution.py:400
  646.2 152.6 %copy-start.16 = (bf16[2,128,1024]{2,1,0:T(8,128)(2,1)}, bf16[2,128,1024]{2,1,0:T(8,128)(2,1)S(1)}, u32[]{:S(2)}) copy-start(bf16[2,128,1024]{2,1,0:T(8,128)(2,1)S(1)} %copy.91) | copy-start | bytes 1572868
  798.8 0.7 copy-start.42
  799.5 8.3 copy-start.11
  799.5 8.4 copy-start.17
  807.9 5.1 copy-start.39
  808.0 5.7 copy-start.6
  808.0 5.7 copy-start.37
  813.0 2.0 copy-start.34
  813.0 2.0 copy-start.35
  813.0 2.0 copy-start.40
  813.0 2.0 copy-start.41
Sparse Core Ops, SparseCore 0:
  10.9 72.2 all-gather.6
  89.7 125.4 all-gather.8
  218.0 54.6 all-gather.10
  275.4 76.3 all-gather.12
  354.4 76.0 all-gather.14
  613.9 177.1 reduce-scatter.5
  793.9 140.4 reduce-scatter.9
  937.3 177.0 reduce-scatter.13
  1117.3 184.0 reduce-scatter.11
  1307.8 158.3 reduce-scatter.7
where the time goes:
time: 1480 us; the launch traced here: 1470 us
  waiting for transfers between devices  956 us (65%)
  matrix products  191 us (13%)
  local copies, waits for them, and re-layouts  134 us (9%)
  blocking collectives  123 us (8%)
  other arithmetic  52.9 us (4%)
  between operations  15.1 us (1%)
    reduce_scatter x1, waiting for transfers between devices, on_device(): lax.psum_scatter(g_w_expand, ('leaf', 'tok'), scatter_dimension=0, tiled=...  187 us
    reduce_scatter x1, waiting for transfers between devices, on_device(): lax.psum_scatter(down_weight_gradient, ('leaf', 'tok'), scatter_dimension...  180 us
    reduce_scatter x1, waiting for transfers between devices, on_device(): lax.psum_scatter(g_w_mixed, ('leaf', 'tok'), scatter_dimension=0, tiled=T...  165 us
    reduce_scatter x1, waiting for transfers between devices, on_device(): lax.psum_scatter(key_grads.astype(jnp.bfloat16), 'tok', scatter_dimension...  145 us
    all_gather x1, waiting for transfers between devices, on_device(): gathered = lax.all_gather(own_pairs, 'tok', axis=1, tiled=True)  83.2 us
    unnamed x2, blocking collectives  82.9 us
    reduce_scatter x1, waiting for transfers between devices, on_device(): lax.psum_scatter(g_w_output, ('leaf', 'tok'), scatter_dimension=0, tiled=...  74.3 us
    all_gather x1, waiting for transfers between devices, on_device(): lax.all_gather(fc2_weight, ('leaf', 'tok'), axis=0, tiled=True)  70.9 us
  transfers between devices with their start and end apart: 10, of which 9 were waited for; matrix products, arithmetic and copies ran while one was open for 13% of the time, Pallas kernels for 0%

commit v1 on v0

v1 whole, which is shorter than its diff:
```python
import jax
import jax.numpy as jnp
from jax import lax
from jax.experimental import pallas as pl
from jax.experimental.pallas import tpu as pltpu
from jax.sharding import PartitionSpec as P

HEADS = 16
UNITS = 16
LOG2E = 1.4426950408889634

layer_eps = 1e-05
masked_score = -1e30
f32 = jnp.float32
bf16 = jnp.bfloat16


def normalize(values):
    row_mean = jnp.mean(values, axis=-1, keepdims=True)
    centered = values - row_mean
    spread = jnp.mean(centered * centered, axis=-1, keepdims=True)
    inverse = lax.rsqrt(spread + layer_eps)
    return centered * inverse, inverse


def norm_back(hat, inverse, gain, grad):
    scaled = grad * gain
    first = jnp.mean(scaled, axis=-1, keepdims=True)
    second = jnp.mean(scaled * hat, axis=-1, keepdims=True)
    return (scaled - first - hat * second) * inverse


def unit_pieces(unit_kind, unit_len):
    if unit_kind < 4:
        return unit_kind
    return 4


def fill_units(pos_ref, qkv_ref, scratches, width):
    blocks, rows, _ = qkv_ref.shape
    for i in range(blocks):
        dst = pl.ds(pl.multiple_of(pos_ref[i], rows), rows)
        for n, scratch in enumerate(scratches):
            scratch[dst, :] = qkv_ref[i, :, n * width : (n + 1) * width]


def fill_transposed(src, dst, unit_len):
    for u in range(UNITS):
        dst[:, u * unit_len : (u + 1) * unit_len] = (
            src[u * unit_len : (u + 1) * unit_len, :].astype(f32).T.astype(bf16)
        )


def head_stack(block, heads, head_size):
    if heads == 1:
        return block
    lane = lax.broadcasted_iota(jnp.int32, block.shape, 1) // head_size
    return jnp.concatenate(
        [jnp.where(lane == h, block, jnp.zeros_like(block)) for h in range(heads)], axis=0
    )


def fill_bias(slope_ref, bias_ref, heads, unit_len):
    depth = lax.broadcasted_iota(jnp.int32, (bias_ref.shape[0], unit_len), 0).astype(f32)
    for h in range(heads):
        bias_ref[:, h * unit_len : (h + 1) * unit_len] = depth * slope_ref[h]


def nt_dot(left, right):
    return lax.dot_general(left, right, (((1,), (1,)), ((), ())), preferred_element_type=f32)


def nn_dot(left, right):
    return lax.dot_general(left, right, (((1,), (0,)), ((), ())), preferred_element_type=f32)


def diag_of(wide, heads, head_size, unit_len):
    return jnp.concatenate(
        [
            wide[h * head_size : (h + 1) * head_size, h * unit_len : (h + 1) * unit_len]
            for h in range(heads)
        ],
        axis=0,
    )


def over_units(unit_len, one_unit):
    for u in range(4):
        pieces = [(u * unit_len, unit_len, u * unit_len, True)]
        if u:
            pieces = [(0, u * unit_len, 0, False)] + pieces
        one_unit(u * unit_len, pieces)

    def branch(b, carry):
        start = pl.multiple_of((4 + b) * unit_len, unit_len)
        one_unit(
            start, [(0, 4 * unit_len, 0, False), (start, unit_len, 4 * unit_len, True)]
        )
        return carry

    lax.fori_loop(0, 4, branch, 0)

    def leaf(k, carry):
        start = pl.multiple_of((8 + k) * unit_len, unit_len)
        parent = pl.multiple_of((4 + k // 2) * unit_len, unit_len)
        one_unit(
            start,
            [
                (0, 4 * unit_len, 0, False),
                (parent, unit_len, 4 * unit_len, False),
                (start, unit_len, 5 * unit_len, True),
            ],
        )
        return carry

    lax.fori_loop(0, 8, leaf, 0)


def forward_kernel(
    pos_ref, out_pos_ref, slope_ref, qkv_ref, ctx_ref, log_ref, q_s, k_s, v_s, vt_s, bias_s, c_s,
    *, heads, head_size
):
    width = heads * head_size
    unit_len = q_s.shape[0] // UNITS
    blocks, rows, _ = qkv_ref.shape
    fill_units(pos_ref, qkv_ref, (q_s, k_s, v_s), width)
    fill_transposed(v_s, vt_s, unit_len)
    fill_bias(slope_ref, bias_s, heads, unit_len)
    scale = head_size ** (-0.5) * LOG2E
    columns = heads * unit_len
    key_row = lax.broadcasted_iota(jnp.int32, (unit_len, columns), 0)
    query_col = lax.broadcasted_iota(jnp.int32, (unit_len, columns), 1) % unit_len
    causal = key_row <= query_col

    def one_unit(start, pieces):
        stacked = head_stack(q_s[pl.ds(start, unit_len), :], heads, head_size)
        scores = []
        top = None
        for key_start, size, depth, diagonal in pieces:
            s = nt_dot(k_s[pl.ds(key_start, size), :], stacked) * scale
            s = s + bias_s[depth : depth + size, :]
            if diagonal:
                s = jnp.where(causal, s, masked_score)
            scores.append(s)
            m = jnp.max(s, axis=0, keepdims=True)
            top = m if top is None else jnp.maximum(top, m)
        total = None
        wide = None
        for (key_start, size, depth, diagonal), s in zip(pieces, scores):
            p = jnp.exp2(s - top)
            part = jnp.sum(p, axis=0, keepdims=True)
            total = part if total is None else total + part
            o = nn_dot(vt_s[:, pl.ds(key_start, size)], p.astype(bf16))
            wide = o if wide is None else wide + o
        wide = wide * (1.0 / total)
        log_ref[pl.ds(start // unit_len, 1), :] = top + jnp.log2(total)
        c_s[pl.ds(start, unit_len), :] = diag_of(wide, heads, head_size, unit_len).T.astype(bf16)

    over_units(unit_len, one_unit)
    for i in range(blocks):
        src = pl.ds(pl.multiple_of(pos_ref[i], rows), rows)
        ctx_ref[out_pos_ref[i], :, :] = c_s[src, :]


def backward_kernel(
    pos_ref, out_pos_ref, slope_ref, qkv_ref, log_ref, gctx_ref, out_ref,
    q_s, k_s, v_s, kt_s, g_s, bias_s, dq_s, dk_s, dv_s, *, heads, head_size
):
    width = heads * head_size
    unit_len = q_s.shape[0] // UNITS
    blocks, rows, _ = qkv_ref.shape
    fill_units(pos_ref, qkv_ref, (q_s, k_s, v_s), width)
    for i in range(blocks):
        dst = pl.ds(pl.multiple_of(pos_ref[i], rows), rows)
        g_s[dst, :] = gctx_ref[out_pos_ref[i], :, :]
    fill_transposed(k_s, kt_s, unit_len)
    fill_bias(slope_ref, bias_s, heads, unit_len)
    dk_s[...] = jnp.zeros_like(dk_s)
    dv_s[...] = jnp.zeros_like(dv_s)
    size_scale = head_size ** (-0.5)
    scale = size_scale * LOG2E
    columns = heads * unit_len
    key_row = lax.broadcasted_iota(jnp.int32, (unit_len, columns), 0)
    query_col = lax.broadcasted_iota(jnp.int32, (unit_len, columns), 1) % unit_len
    causal = key_row <= query_col

    def one_unit(start, pieces):
        stacked = head_stack(q_s[pl.ds(start, unit_len), :], heads, head_size)
        grads = head_stack(g_s[pl.ds(start, unit_len), :], heads, head_size)
        log_total = log_ref[pl.ds(start // unit_len, 1), :]
        kept = []
        delta = None
        for key_start, size, depth, diagonal in pieces:
            s = nt_dot(k_s[pl.ds(key_start, size), :], stacked) * scale
            s = s + bias_s[depth : depth + size, :]
            if diagonal:
                s = jnp.where(causal, s, masked_score)
            p = jnp.exp2(s - log_total)
            gp = nt_dot(v_s[pl.ds(key_start, size), :], grads)
            kept.append((p, gp))
            part = jnp.sum(p * gp, axis=0, keepdims=True)
            delta = part if delta is None else delta + part
        wide = None
        for (key_start, size, depth, diagonal), (p, gp) in zip(pieces, kept):
            ds = (p * (gp - delta)).astype(bf16)
            keys = pl.ds(key_start, size)
            dv_s[keys, :] += nn_dot(p.astype(bf16), grads)
            dk_s[keys, :] += nn_dot(ds, stacked)
            o = nn_dot(kt_s[:, keys], ds)
            wide = o if wide is None else wide + o
        dq = diag_of(wide, heads, head_size, unit_len).T * size_scale
        dq_s[pl.ds(start, unit_len), :] = dq.astype(bf16)

    over_units(unit_len, one_unit)
    for i in range(blocks):
        src = pl.ds(pl.multiple_of(pos_ref[i], rows), rows)
        out_ref[i, :, :width] = dq_s[src, :]
        out_ref[i, :, width : 2 * width] = (dk_s[src, :] * size_scale).astype(bf16)
        out_ref[i, :, 2 * width :] = dv_s[src, :].astype(bf16)


def attention_forward(pos, out_pos, slopes, qkv, heads, head_size):
    blocks, rows, _ = qkv.shape
    tokens, width = blocks * rows, heads * head_size
    unit_len = tokens // UNITS
    smem = pl.BlockSpec(memory_space=pltpu.SMEM)
    vmem = pl.BlockSpec(memory_space=pltpu.VMEM)
    seq = lambda: pltpu.VMEM((tokens, width), bf16)
    return pl.pallas_call(
        lambda *refs: forward_kernel(*refs, heads=heads, head_size=head_size),
        out_shape=(
            jax.ShapeDtypeStruct((blocks, rows, width), bf16),
            jax.ShapeDtypeStruct((UNITS, heads * unit_len), f32),
        ),
        in_specs=[smem, smem, smem, vmem],
        out_specs=(vmem, vmem),
        scratch_shapes=[
            seq(), seq(), seq(), pltpu.VMEM((width, tokens), bf16),
            pltpu.VMEM((6 * unit_len, heads * unit_len), f32), seq(),
        ],
        compiler_params=pltpu.CompilerParams(vmem_limit_bytes=24 * 2**20),
        cost_estimate=pl.CostEstimate(
            flops=tokens * tokens * width * 2, bytes_accessed=tokens * width * 16,
            transcendentals=tokens * tokens * heads // 3,
        ),
    )(pos, out_pos, slopes, qkv)


def attention_backward(pos, out_pos, slopes, qkv, log_total, gctx, heads, head_size):
    blocks, rows, _ = qkv.shape
    tokens, width = blocks * rows, heads * head_size
    unit_len = tokens // UNITS
    smem = pl.BlockSpec(memory_space=pltpu.SMEM)
    vmem = pl.BlockSpec(memory_space=pltpu.VMEM)
    seq = lambda: pltpu.VMEM((tokens, width), bf16)
    acc = lambda: pltpu.VMEM((tokens, width), f32)
    return pl.pallas_call(
        lambda *refs: backward_kernel(*refs, heads=heads, head_size=head_size),
        out_shape=jax.ShapeDtypeStruct((blocks, rows, 3 * width), bf16),
        in_specs=[smem, smem, smem, vmem, vmem, vmem],
        out_specs=vmem,
        scratch_shapes=[
            seq(), seq(), seq(), pltpu.VMEM((width, tokens), bf16), seq(),
            pltpu.VMEM((6 * unit_len, heads * unit_len), f32), seq(), acc(), acc(),
        ],
        compiler_params=pltpu.CompilerParams(vmem_limit_bytes=32 * 2**20),
        cost_estimate=pl.CostEstimate(
            flops=tokens * tokens * width * 5, bytes_accessed=tokens * width * 30,
            transcendentals=tokens * tokens * heads // 3,
        ),
    )(pos, out_pos, slopes, qkv, log_total, gctx)


def swap(values, axis, mask):
    size = lax.axis_size(axis)
    return lax.ppermute(values, axis, [(i, i ^ mask) for i in range(size)])


def masks_of(size):
    found, mask = [], 1
    while mask < size:
        found.append(mask)
        mask *= 2
    return found


def grow(values, axis, masks):
    index = lax.axis_index(axis)
    for mask in masks:
        other = swap(values, axis, mask)
        high = (index & mask) != 0
        values = jnp.concatenate(
            [jnp.where(high, other, values), jnp.where(high, values, other)], axis=0
        )
    return values


def shrink(values, axis, masks):
    index = lax.axis_index(axis)
    for mask in reversed(masks):
        half = values.shape[0] // 2
        low, high = values[:half], values[half:]
        upper = (index & mask) != 0
        other = swap(jnp.where(upper, low, high), axis, mask)
        values = (
            jnp.where(upper, high, low).astype(f32) + other.astype(f32)
        ).astype(values.dtype)
    return values


def block_order(ranks):
    far = [m for m in masks_of(ranks) if m > 1]
    order = []
    for half, masks in ((0, far), (1, far[::-1])):
        seen = [0]
        for m in masks:
            seen = seen + [j ^ m for j in seen]
        order += [(j, half) for j in seen]
    return order + [(j ^ 1, half) for j, half in order]


def gather_blocks(pair, ranks):
    far = [m for m in masks_of(ranks) if m > 1]
    halves = []
    for half, masks in ((0, far), (1, far[::-1])):
        held = pair[half : half + 1]
        for m in masks:
            held = jnp.concatenate([held, swap(held, "tok", m)], axis=0)
        halves.append(held)
    held = jnp.concatenate(halves, axis=0)
    return jnp.concatenate([held, swap(held, "tok", 1)], axis=0)


def scatter_blocks(partial, ranks):
    far = [m for m in masks_of(ranks) if m > 1]
    n = partial.shape[0] // 2
    other = swap(partial[n:].astype(bf16), "tok", 1)
    held = partial[:n].astype(f32) + other.astype(f32)
    done = []
    for half, masks in ((0, far), (1, far[::-1])):
        part = held[half * (n // 2) : (half + 1) * (n // 2)]
        for m in masks[::-1]:
            k = part.shape[0] // 2
            part = part[:k] + swap(part[k:].astype(bf16), "tok", m).astype(f32)
        done.append(part)
    return jnp.concatenate(done, axis=0)


def on_device(
    hidden_in, output_cotangent, unit_place, ln1_gain, ln1_bias, qkv_weight, qv_bias, out_weight,
    out_bias, ln2_gain, ln2_bias, fc1_weight, fc1_bias, fc2_weight, fc2_bias,
):
    trees, rows, width = hidden_in.shape
    tok_size, leaf_size = lax.axis_size("tok"), lax.axis_size("leaf")
    ranks = tok_size // trees
    head_size = width // HEADS
    heads = HEADS // ranks
    lanes = heads * head_size
    hidden_units = fc1_weight.shape[1]
    own_units = fc1_bias.shape[0]
    weight_rows = qkv_weight.shape[0]
    groups = leaf_size * trees
    tokens = rows * tok_size
    unit_len = tokens // UNITS
    leaf_masks, tree_masks = masks_of(leaf_size), [m * ranks for m in masks_of(trees)]
    index = lax.axis_index("tok")
    tree, rank = index // ranks, index % ranks
    rank_groups = [[g * ranks + i for i in range(ranks)] for g in range(trees)]

    def exchange(values):
        mine = jnp.where(tree == 0, values[0], values[1])
        other = swap(jnp.where(tree == 0, values[1], values[0]), "tok", ranks)
        return jnp.stack([jnp.where(tree == 0, mine, other), jnp.where(tree == 0, other, mine)])

    def to_ranks(values):
        return lax.all_to_all(
            values, "tok", 0, 0, tiled=True, axis_index_groups=rank_groups
        )

    def spread(values):
        return grow(grow(values[None], "tok", tree_masks), "leaf", leaf_masks)

    def collect(values):
        return shrink(shrink(values, "leaf", leaf_masks), "tok", tree_masks)[0]

    order = block_order(ranks)
    dist = jnp.array([j for j, _ in order], jnp.int32)
    half = jnp.array([h for _, h in order], jnp.int32)
    peer = rank ^ dist
    position = (half * ranks + peer) * rows
    place = jnp.where(tree == 0, unit_place[0], unit_place[1])
    slot = position // unit_len
    unit_at = jnp.sum(
        jnp.where(slot[:, None] == jnp.arange(UNITS, dtype=jnp.int32)[None, :], place[None, :], 0),
        axis=1,
    )
    pos = unit_at * unit_len + position % unit_len
    out_pos = peer * 2 + half
    head_index = (rank * heads + jnp.arange(heads, dtype=jnp.int32)).astype(f32)
    slopes = jnp.exp2(-8.0 * (head_index + 1.0) / HEADS) * LOG2E

    hidden = exchange(hidden_in)
    hidden_all = gather_blocks(hidden, ranks)

    small = jnp.concatenate(
        [ln1_gain, ln1_bias, qv_bias, out_bias, ln2_gain, ln2_bias, fc1_bias, fc2_bias]
    )
    mixed_cols = 3 * lanes
    small_rows = -(-small.shape[0] // mixed_cols)
    small_block = jnp.pad(small, (0, small_rows * mixed_cols - small.shape[0]))
    small_block = jnp.broadcast_to(
        small_block.reshape(1, small_rows, mixed_cols), (ranks, small_rows, mixed_cols)
    )
    mixed_parts = (
        qkv_weight.reshape(weight_rows, 3, ranks, lanes)
        .transpose(2, 0, 1, 3)
        .reshape(ranks, weight_rows, mixed_cols)
    )
    up_cols = groups * own_units
    up_parts = (
        fc1_weight.reshape(weight_rows, groups, ranks, own_units)
        .transpose(2, 0, 1, 3)
        .reshape(ranks, weight_rows, up_cols)
    )
    mixed_sent = to_ranks(jnp.concatenate([mixed_parts, small_block], axis=1))
    up_sent = to_ranks(up_parts)
    mixed_all = spread(mixed_sent)
    w_mixed = mixed_all[:, :, :weight_rows].reshape(width, mixed_cols)
    smalls = mixed_all[:, :, weight_rows:].reshape(groups * ranks, small_rows * mixed_cols)
    up_weight = spread(up_sent).reshape(width, up_cols)
    down_weight = spread(fc2_weight).reshape(up_cols, width)
    w_output = lax.all_gather(out_weight, ("leaf", "tok"), axis=0, tiled=True)

    def small_of(start, array):
        n = array.shape[0]
        return smalls[:, start : start + n].reshape(-1).astype(f32), start + n

    gain_one, at = small_of(0, ln1_gain)
    shift_one, at = small_of(at, ln1_bias)
    bias_mixed, at = small_of(at, qv_bias)
    bias_output, at = small_of(at, out_bias)
    gain_two, at = small_of(at, ln2_gain)
    shift_two, at = small_of(at, ln2_bias)
    bias_up, at = small_of(at, fc1_bias)
    bias_down, at = small_of(at, fc2_bias)
    own_bias_up = lax.dynamic_index_in_dim(
        bias_up.reshape(groups, ranks, own_units), rank, 1, keepdims=False
    ).reshape(up_cols)
    query_bias = lax.dynamic_slice_in_dim(bias_mixed, rank * lanes, lanes)
    value_bias = lax.dynamic_slice_in_dim(bias_mixed, width + rank * lanes, lanes)

    cotangent = exchange(output_cotangent)
    cotangent_all = gather_blocks(cotangent, ranks)

    hat_one, inverse_one = normalize(hidden_all.astype(f32))
    normed_one = (hat_one * gain_one + shift_one).astype(bf16)
    projected = jnp.einsum("brd,de->bre", normed_one, w_mixed, preferred_element_type=f32)
    qkv_bias = jnp.concatenate([query_bias, jnp.zeros((lanes,), f32), value_bias])
    qkv = (projected + qkv_bias).astype(bf16)
    ctx_sent, log_total = attention_forward(pos, out_pos, slopes, qkv, heads, head_size)
    ctx_parts = to_ranks(ctx_sent.reshape(ranks, 2 * rows, lanes))
    context = ctx_parts.transpose(1, 0, 2).reshape(2, rows, width)

    branch_out = jnp.einsum("mrd,de->mre", context, w_output, preferred_element_type=f32)
    middle = hidden.astype(f32) + (branch_out + bias_output)
    hat_two, inverse_two = normalize(middle)
    normed_two = (hat_two * gain_two + shift_two).astype(bf16)
    normed_all = gather_blocks(normed_two, ranks)

    expand = jnp.einsum("brd,df->brf", normed_all, up_weight, preferred_element_type=f32)
    expand = expand + own_bias_up
    root = (2.0 / jnp.pi) ** 0.5
    square = expand * expand
    tanh = jnp.tanh(root * (expand + 0.044715 * square * expand))
    active = (0.5 * expand * (1.0 + tanh)).astype(bf16)
    slope = 0.5 * (1.0 + tanh) + 0.5 * expand * (1.0 - tanh * tanh) * root * (
        1.0 + 3 * 0.044715 * square
    )
    grad_active = jnp.einsum("brd,fd->brf", cotangent_all, down_weight, preferred_element_type=f32)
    grad_expand = (grad_active * slope).astype(bf16)
    grad_normed_part = jnp.einsum(
        "brf,df->brd", grad_expand, up_weight, preferred_element_type=f32
    ).astype(bf16)
    grad_normed_two = scatter_blocks(grad_normed_part, ranks)

    reduced_part = jnp.einsum(
        "brf,fd->brd", active, down_weight, preferred_element_type=f32
    ).astype(bf16)
    reduced = scatter_blocks(reduced_part, ranks)
    layer_out = exchange((middle + (reduced + bias_down)).astype(bf16))

    g_down = jnp.einsum("brf,brd->fd", active, cotangent_all, preferred_element_type=f32)
    g_up = jnp.einsum("brd,brf->df", normed_all, grad_expand, preferred_element_type=f32)
    g_bias_up = jnp.sum(grad_expand, axis=(0, 1), dtype=f32)
    g_down_own = collect(g_down.reshape(groups, own_units, width).astype(bf16)).astype(f32)
    g_up_parts = collect(g_up.reshape(groups, ranks, weight_rows, up_cols).astype(bf16))
    g_up_own = (
        to_ranks(g_up_parts)
        .reshape(ranks, weight_rows, groups, own_units)
        .transpose(1, 2, 0, 3)
        .reshape(weight_rows, hidden_units)
        .astype(f32)
    )

    cot = cotangent.astype(f32)
    g_gain_two = jnp.sum(grad_normed_two * hat_two, axis=(0, 1))
    g_shift_two = jnp.sum(grad_normed_two, axis=(0, 1))
    g_bias_down = jnp.sum(cot, axis=(0, 1))
    grad_middle = cot + norm_back(hat_two, inverse_two, gain_two, grad_normed_two)
    grad_branch = grad_middle.astype(bf16)
    g_bias_output = jnp.sum(grad_branch, axis=(0, 1), dtype=f32)
    grad_context = jnp.einsum(
        "mre,de->mrd", grad_branch, w_output, preferred_element_type=f32
    ).astype(bf16)
    gctx_sent = grad_context.reshape(2 * rows, ranks, lanes).transpose(1, 0, 2)
    gctx_parts = to_ranks(gctx_sent).reshape(2 * ranks, rows, lanes)
    g_output = jnp.einsum("mrd,mre->de", context, grad_branch, preferred_element_type=f32)
    g_output_own = lax.psum_scatter(
        g_output.astype(bf16), ("leaf", "tok"), scatter_dimension=0, tiled=True
    ).astype(f32)

    grad_projected = attention_backward(
        pos, out_pos, slopes, qkv, log_total, gctx_parts, heads, head_size
    )
    grad_normed_one = jnp.einsum(
        "bre,de->brd", grad_projected, w_mixed, preferred_element_type=f32
    )
    g_gain_one = jnp.sum(grad_normed_one * hat_one, axis=(0, 1))
    g_shift_one = jnp.sum(grad_normed_one, axis=(0, 1))
    grad_one = scatter_blocks(grad_normed_one.astype(bf16), ranks)
    hat_own, inverse_own = normalize(hidden.astype(f32))
    input_grad = exchange(
        (grad_middle + norm_back(hat_own, inverse_own, gain_one, grad_one)).astype(bf16)
    )

    g_mixed = jnp.einsum("brd,bre->de", normed_one, grad_projected, preferred_element_type=f32)
    g_bias_mixed = jnp.sum(grad_projected, axis=(0, 1), dtype=f32)
    own_lane = jnp.arange(ranks, dtype=jnp.int32)[:, None] == rank
    g_bias_query = jnp.where(own_lane, g_bias_mixed[None, :lanes], 0.0).reshape(-1)
    g_bias_value = jnp.where(own_lane, g_bias_mixed[None, 2 * lanes :], 0.0).reshape(-1)
    g_bias_up_all = jnp.where(
        own_lane[None], g_bias_up.reshape(groups, 1, own_units), 0.0
    ).reshape(-1)
    pieces = [
        g_gain_one, g_shift_one, jnp.concatenate([g_bias_query, g_bias_value]), g_bias_output,
        g_gain_two, g_shift_two, g_bias_up_all, g_bias_down,
    ]
    sizes = [p.shape[0] // (groups * ranks) for p in pieces]
    g_small = jnp.concatenate([p.reshape(groups, ranks, -1) for p in pieces], axis=2)
    g_small = jnp.pad(g_small, ((0, 0), (0, 0), (0, small_rows * mixed_cols - g_small.shape[2])))
    g_sent = jnp.concatenate(
        [
            g_mixed.reshape(groups, ranks, weight_rows, mixed_cols),
            g_small.reshape(groups, ranks, small_rows, mixed_cols),
        ],
        axis=2,
    ).astype(bf16)
    g_back = to_ranks(collect(g_sent))
    g_mixed_own = (
        g_back[:, :weight_rows]
        .reshape(ranks, weight_rows, 3, lanes)
        .transpose(1, 2, 0, 3)
        .reshape(weight_rows, 3 * width)
        .astype(f32)
    )
    small_sum = jnp.sum(g_back[:, weight_rows:].astype(f32), axis=0).reshape(-1)
    found, at = [], 0
    for size in sizes:
        found.append(small_sum[at : at + size])
        at += size
    (
        o_gain_one, o_shift_one, o_bias_mixed, o_bias_output, o_gain_two, o_shift_two, o_bias_up,
        o_bias_down,
    ) = found
    return (
        layer_out, input_grad, o_gain_one, o_shift_one, g_mixed_own, o_bias_mixed, g_output_own,
        o_bias_output, o_gain_two, o_shift_two, g_up_own, o_bias_up, g_down_own, o_bias_down,
    )


def solution(mesh):
    both = ("leaf", "tok")
    tokens, matrix, vector = P("leaf", "tok", None), P(both, None), P(both)
    return jax.shard_map(
        on_device,
        mesh=mesh,
        in_specs=(
            tokens, tokens, P("leaf", None), vector, vector, matrix, vector, matrix, vector, vector,
            vector, matrix, vector, matrix, vector,
        ),
        out_specs=(
            tokens, tokens, vector, vector, matrix, vector, matrix, vector, vector, vector, matrix,
            vector, matrix, vector,
        ),
        check_vma=False,
    )
```

time: 1480 us -> 531 us (0.36)
  waiting for transfers between devices: 956 us -> 251 us
  matrix products: 191 us -> 37.5 us
  blocking collectives: 123 us -> 0 us
  starting transfers between devices: 0.57 us -> 83.3 us
  local copies, waits for them, and re-layouts: 134 us -> 54.2 us
  Pallas kernels: 0 us -> 24.8 us
    reduce_scatter x5 -> x1, waiting for transfers between devices: 751 us -> 52.2 us  [on_device(): lax.psum_scatter(g_output.astype(bf16), ('leaf', 'tok'), scatter_dimensio...]
    all_gather x5 -> x1, waiting for transfers between devices: 203 us -> 0.01 us  [on_device(): w_output = lax.all_gather(out_weight, ('leaf', 'tok'), axis=0, tiled=True)]
    ppermute x0 -> x46, waiting for transfers between devices: none -> 193 us  [swap(): return lax.ppermute(values, axis, [(i, i ^ mask) for i in range(size)])]
    dot_general x48 -> x12, matrix products: 191 us -> 37.5 us  [the longest x1 5.06 us: on_device(): jnp.einsum('brd,fd->brf', cotangent_all, down_weight, preferred_element_t...]
    unnamed x2 -> x0, blocking collectives: 82.9 us -> none
    ppermute x0 -> x46, starting transfers between devices: none -> 60.2 us  [swap(): return lax.ppermute(values, axis, [(i, i ^ mask) for i in range(size)])]
    dynamic_update_slice x8 -> x0, local copies, waits for them, and re-layouts: 44.1 us -> none  [grad_pass(): lax.dynamic_update_slice_in_dim(key_grads, block_piece, block_index * blo...]
    all_gather x1 -> x0, blocking collectives: 39.7 us -> none  [on_device(): lax.all_gather(fc1_bias, ('leaf', 'tok'), axis=0, tiled=True)]
  transfers between devices with their start and end apart: 10 -> 54, of which waited for: 9 -> 27; matrix products, arithmetic and copies ran while one was open for 13% -> 23% of each run, Pallas kernels for 0% -> 5%
where the time goes in v1:
time: 531 us; the launch traced here: 521 us
  waiting for transfers between devices  251 us (47%)
  starting transfers between devices  83.3 us (16%)
  other arithmetic  55.1 us (10%)
  local copies, waits for them, and re-layouts  54.2 us (10%)
  matrix products  37.5 us (7%)
  Pallas kernels  24.8 us (5%)
  between operations  15.7 us (3%)
    ppermute x46, waiting for transfers between devices, swap(): return lax.ppermute(values, axis, [(i, i ^ mask) for i in range(size)])  193 us
    ppermute x46, starting transfers between devices, swap(): return lax.ppermute(values, axis, [(i, i ^ mask) for i in range(size)])  60.2 us
    reduce_scatter x1, waiting for transfers between devices, on_device(): lax.psum_scatter(g_output.astype(bf16), ('leaf', 'tok'), scatter_dimensio...  52.2 us
    unnamed x131, local copies, waits for them, and re-layouts  29.3 us
    all_to_all x6, starting transfers between devices, to_ranks(): lax.all_to_all(values, 'tok', 0, 0, tiled=True, axis_index_groups=rank_gr...  23 us
    pallas_call x1, Pallas kernels, attention_backward(): pl.pallas_call(lambda *refs: backward_kernel(*refs, heads=heads, head_siz...  12.7 us
    pallas_call x1, Pallas kernels, attention_forward(): pl.pallas_call(lambda *refs: forward_kernel(*refs, heads=heads, head_size...  12.1 us
  transfers between devices with their start and end apart: 54, of which 27 were waited for; matrix products, arithmetic and copies ran while one was open for 23% of the time, Pallas kernels for 5%

profile of v1, /device:TPU:0, one launch (start us, length us, event | category | flops | bytes accessed | tf_op | source)
XLA Modules:
  0.0 521.4 jit_solution(6591049208669619257)
XLA Ops:
  8.4 4.1 collective-permute-start
  12.5 11.9 %collective-permute-done = bf16[128,1024]{1,0:T(8,128)(2,1)S(1)} collective-permute-done((bf16[128,1024]{1,0:T(8,128)(2,1)S(1)}, bf16[128,1024]{1,0:T(8,128)(2,1)S(1)}, u32[]{:S(2)}, u32[]{:S(2)}) %collective-permute-start) | collective-permute-done | bytes 262176 | tf_op jit(solution)/shard_map/ppermute | solution.py:276
  27.2 6.0 %collective-permute-done.1 = bf16[1,128,1024]{2,1,0:T(8,128)(2,1)S(1)} collective-permute-done((bf16[1,128,1024]{2,1,0:T(8,128)(2,1)S(1)}, bf16[1,128,1024]{2,1,0:T(8,128)(2,1)S(1)}, u32[]{:S(2)}, u32[]{:S(2)}) %collective-permute-start.1) | collective-permute-done | bytes 262176 | tf_op jit(solution)/shard_map/ppermute | solution.py:276
  36.3 9.8 %collective-permute-done.2 = bf16[2,128,1024]{2,1,0:T(8,128)(2,1)S(1)} collective-permute-done((bf16[2,128,1024]{2,1,0:T(8,128)(2,1)S(1)}, bf16[2,128,1024]{2,1,0:T(8,128)(2,1)S(1)}, u32[]{:S(2)}, u32[]{:S(2)}) %collective-permute-start.2) | collective-permute-done | bytes 524320 | tf_op jit(solution)/shard_map/ppermute | solution.py:276
  50.3 3.4 all-to-all-start
  53.8 1.9 collective-permute-start.4
  55.8 3.4 collective-permute-start.23
  59.9 3.4 collective-permute-start.6
  64.9 5.7 %collective-permute-done.4 = bf16[2,128,1024]{2,1,0:T(8,128)(2,1)S(1)} collective-permute-done((bf16[2,128,1024]{2,1,0:T(8,128)(2,1)S(1)}, bf16[2,128,1024]{2,1,0:T(8,128)(2,1)S(1)}, u32[]{:S(2)}, u32[]{:S(2)}) %collective-permute-start.4) | collective-permute-done | bytes 524320 | tf_op jit(solution)/shard_map/ppermute | solution.py:276
  71.8 22.7 %collective-permute-done.6 = bf16[1,8,33,384]{3,2,1,0:T(8,128)(2,1)} collective-permute-done((bf16[1,8,33,384]{3,2,1,0:T(8,128)(2,1)S(1)}, bf16[1,8,33,384]{3,2,1,0:T(8,128)(2,1)}, u32[]{:S(2)}, u32[]{:S(2)}) %collective-permute-start.6) | collective-permute-done | bytes 202784 | tf_op jit(solution)/shard_map/ppermute | solution.py:276
  97.4 11.6 %collective-permute-done.7 = bf16[2,8,33,384]{3,2,1,0:T(8,128)(2,1)S(1)} collective-permute-done((bf16[2,8,33,384]{3,2,1,0:T(8,128)(2,1)S(1)}, bf16[2,8,33,384]{3,2,1,0:T(8,128)(2,1)S(1)}, u32[]{:S(2)}, u32[]{:S(2)}) %collective-permute-start.7) | collective-permute-done | bytes 405536 | tf_op jit(solution)/shard_map/ppermute | solution.py:276
  109.8 3.4 constant_dynamic-update-slice_fusion.6
  113.2 2.8 convert_reduce_fusion
  116.1 3.2 fusion.7
  119.3 4.9 add_convert_fusion.refs_3_
  124.2 12.1 %shard_map.272 = (bf16[16,128,128]{2,1,0:T(8,128)(2,1)}, f32[16,256]{1,0:T(8,128)S(1)}) custom-call(s32[16]{0:T(128)S(1)} %fusion.63.refs_0_, s32[16]{0:T(128)S(1)} %get-tuple-element.127.refs_1_, f32[2]{0:T(128)S(1)} %exponential_multiply_fusion.refs_2_, bf16[16,128,384]{2,1,0:T(8,128)(2,1)S(1)} %add_convert_fusion.refs_3_), custom_call_target="tpu_custom_call" | custom-call | flops 1073741824 | bytes 4194304 | tf_op jit(solution)/shard_map/pallas_call | solution.py:229
  136.2 4.2 all-to-all-start.1
  148.3 6.5 %collective-permute-done.24 = bf16[1,128,1024]{2,1,0:T(8,128)(2,1)S(1)} collective-permute-done((bf16[1,128,1024]{2,1,0:T(8,128)(2,1)S(1)}, bf16[1,128,1024]{2,1,0:T(8,128)(2,1)S(1)}, u32[]{:S(2)}, u32[]{:S(2)}) %collective-permute-start.24) | collective-permute-done | bytes 262176 | tf_op jit(solution)/shard_map/ppermute | solution.py:276
  158.8 4.2 all-to-all-start.2
  165.5 2.5 fusion.82
  170.1 2.0 collective-permute-start.8
  172.1 2.2 constant_dynamic-update-slice_fusion.29
  176.7 2.1 collective-permute-done.8
  185.4 2.3 collective-permute-start.13
  193.7 6.7 %collective-permute-done.9 = bf16[2,128,1024]{2,1,0:T(8,128)(2,1)} collective-permute-done((bf16[2,128,1024]{2,1,0:T(8,128)(2,1)}, bf16[2,128,1024]{2,1,0:T(8,128)(2,1)}, u32[]{:S(2)}, u32[]{:S(2)}) %collective-permute-start.9) | collective-permute-done | bytes 524320 | tf_op jit(solution)/shard_map/ppermute | solution.py:276
  207.1 4.2 collective-permute-done.10
  213.5 9.9 %collective-permute-done.11 = bf16[2,128,1024]{2,1,0:T(8,128)(2,1)S(1)} collective-permute-done((bf16[2,128,1024]{2,1,0:T(8,128)(2,1)S(1)}, bf16[2,128,1024]{2,1,0:T(8,128)(2,1)S(1)}, u32[]{:S(2)}, u32[]{:S(2)}) %collective-permute-start.11) | collective-permute-done | bytes 524320 | tf_op jit(solution)/shard_map/ppermute | solution.py:276
  231.6 9.9 %collective-permute-done.14 = bf16[2,8,32,512]{3,2,1,0:T(8,128)(2,1)} collective-permute-done((bf16[2,8,32,512]{3,2,1,0:T(8,128)(2,1)}, bf16[2,8,32,512]{3,2,1,0:T(8,128)(2,1)}, u32[]{:S(2)}, u32[]{:S(2)}) %collective-permute-start.14) | collective-permute-done | bytes 524320 | tf_op jit(solution)/shard_map/ppermute | solution.py:276
  246.5 2.3 fusion.83
  248.9 2.9 convolution_convert_fusion.1
  251.8 5.1 convert_reduce_fusion.1
  256.9 2.4 bitcast_convert_fusion.2
  261.1 2.4 convolution_convert_fusion
  265.6 2.5 bitcast_convert_fusion.1
  269.9 2.6 collective-permute-done.42
  280.0 11.6 %collective-permute-done.18 = bf16[2,128,1024]{2,1,0:T(8,128)(2,1)S(1)} collective-permute-done((bf16[2,128,1024]{2,1,0:T(8,128)(2,1)S(1)}, bf16[2,128,1024]{2,1,0:T(8,128)(2,1)S(1)}, u32[]{:S(2)}, u32[]{:S(2)}) %collective-permute-start.18) | collective-permute-done | bytes 524320 | tf_op jit(solution)/shard_map/ppermute | solution.py:276
  293.7 10.5 %collective-permute-done.30 = bf16[2,128,1024]{2,1,0:T(8,128)(2,1)S(1)} collective-permute-done((bf16[2,128,1024]{2,1,0:T(8,128)(2,1)S(1)}, bf16[2,128,1024]{2,1,0:T(8,128)(2,1)S(1)}, u32[]{:S(2)}, u32[]{:S(2)}) %collective-permute-start.30) | collective-permute-done | bytes 524320 | tf_op jit(solution)/shard_map/ppermute | solution.py:276
  304.8 2.1 collective-permute-start.33
  307.0 4.4 collective-permute-done.21
  311.6 2.6 collective-permute-done.33
  315.8 1.9 convert_reduce_fusion.4
  319.4 3.5 all-to-all-start.3
  325.9 2.1 collective-permute-start.45
  328.1 1.9 fusion.46
  330.2 4.7 all-to-all-done.3
  334.9 4.1 all-to-all-start.5
  339.1 12.7 %shard_map.273 = bf16[16,128,384]{2,1,0:T(8,128)(2,1)S(1)} custom-call(s32[16]{0:T(128)S(1)} %fusion.63.refs_0_, s32[16]{0:T(128)S(1)} %get-tuple-element.127.refs_1_, f32[2]{0:T(128)S(1)} %exponential_multiply_fusion.refs_2_, bf16[16,128,384]{2,1,0:T(8,128)(2,1)S(1)} %add_convert_fusion.refs_3_, f32[16,256]{1,0:T(8,128)S(1)} %get-tuple-element.17.refs_4_, ...), custom_call_target="tpu_custom_call" | custom-call | flops 2684354560 | bytes 7864320 | tf_op jit(solution)/shard_map/pallas_call | solution.py:257
  351.8 5.0 bitcast_convert_fusion.3
  357.2 4.6 fusion.70
  361.9 2.0 copy-done.10
  373.1 2.1 bitcast_convert_fusion
  375.2 5.5 %collective-permute-done.40 = bf16[2,8,33,384]{3,2,1,0:T(8,128)(2,1)S(1)} collective-permute-done((bf16[2,8,33,384]{3,2,1,0:T(8,128)(2,1)}, bf16[2,8,33,384]{3,2,1,0:T(8,128)(2,1)S(1)}, u32[]{:S(2)}, u32[]{:S(2)}) %collective-permute-start.40) | collective-permute-done | bytes 405536 | tf_op jit(solution)/shard_map/ppermute | solution.py:276
  382.2 3.0 collective-permute-start.22
  385.2 18.6 %collective-permute-done.41 = bf16[1,8,33,384]{3,2,1,0:T(8,128)(2,1)S(1)} collective-permute-done((bf16[1,8,33,384]{3,2,1,0:T(8,128)(2,1)S(1)}, bf16[1,8,33,384]{3,2,1,0:T(8,128)(2,1)S(1)}, u32[]{:S(2)}, u32[]{:S(2)}) %collective-permute-start.41) | collective-permute-done | bytes 202784 | tf_op jit(solution)/shard_map/ppermute | solution.py:276
  404.6 3.6 all-to-all-start.4
  408.3 5.3 %fusion.69 = (bf16[8,128,1024]{2,1,0:T(8,128)(2,1)S(1)}, f32[8,128,1024]{2,1,0:T(8,128)}) fusion(bf16[8,128,1024]{2,1,0:T(8,128)(2,1)} %collective-permute-done.34, bf16[16,128,1024]{2,1,0:T(8,128)(2,1)} %copy-done.10), kind=kLoop, calls=%fused_computation.261 | loop fusion | flops 4194304 | bytes 10485760 | tf_op jit(solution)/shard_map/convert.40
  414.6 2.0 collective-permute-start.35
  419.0 11.2 %collective-permute-done.35 = bf16[2,128,1024]{2,1,0:T(8,128)(2,1)} collective-permute-done((bf16[2,128,1024]{2,1,0:T(8,128)(2,1)}, bf16[2,128,1024]{2,1,0:T(8,128)(2,1)}, u32[]{:S(2)}, u32[]{:S(2)}) %collective-permute-start.35) | collective-permute-done | bytes 524320 | tf_op jit(solution)/shard_map/ppermute | solution.py:276
  430.2 2.5 collective-permute-done.37
  432.6 2.2 slice_add_fusion.1
  434.9 2.2 collective-permute-start.36
  439.1 3.9 collective-permute-done.36
  448.2 11.4 %collective-permute-done.39 = bf16[128,1024]{1,0:T(8,128)(2,1)S(1)} collective-permute-done((bf16[128,1024]{1,0:T(8,128)(2,1)S(1)}, bf16[128,1024]{1,0:T(8,128)(2,1)S(1)}, u32[]{:S(2)}, u32[]{:S(2)}) %collective-permute-start.39) | collective-permute-done | bytes 262176 | tf_op jit(solution)/shard_map/ppermute | solution.py:276
  460.5 52.2 %reduce-scatter.2.cloned.1.call-done = bf16[32,1024]{1,0:T(8,128)(2,1)} async-done(((bf16[1024,1024]{1,0:T(8,128)(2,1)}), bf16[32,1024]{1,0:T(8,128)(2,1)}) %reduce-scatter.2.cloned.1.call-update) | async-done | bytes 65552 | tf_op jit(solution)/shard_map/reduce_scatter | solution.py:518
  (346 shorter events, 119.0 us)
Async XLA Ops:
  7.2 42.1 %copy-start.38 = (bf16[32]{0:T(256)(128)(2,1)S(1)}, bf16[32]{0:T(256)(128)(2,1)}, u32[]{:S(2)}) copy-start(bf16[32]{0:T(256)(128)(2,1)} %param.20) | copy-start | bytes 196
  7.2 42.1 %copy-start.39 = (bf16[32]{0:T(256)(128)(2,1)S(1)}, bf16[32]{0:T(256)(128)(2,1)}, u32[]{:S(2)}) copy-start(bf16[32]{0:T(256)(128)(2,1)} %param.21) | copy-start | bytes 196
  7.2 42.1 %copy-start.40 = (bf16[64]{0:T(256)(128)(2,1)S(1)}, bf16[64]{0:T(256)(128)(2,1)}, u32[]{:S(2)}) copy-start(bf16[64]{0:T(256)(128)(2,1)} %param.23) | copy-start | bytes 388
  7.3 42.1 %copy-start.41 = (bf16[32]{0:T(256)(128)(2,1)S(1)}, bf16[32]{0:T(256)(128)(2,1)}, u32[]{:S(2)}) copy-start(bf16[32]{0:T(256)(128)(2,1)} %param.25) | copy-start | bytes 196
  7.3 42.1 %copy-start.42 = (bf16[32]{0:T(256)(128)(2,1)S(1)}, bf16[32]{0:T(256)(128)(2,1)}, u32[]{:S(2)}) copy-start(bf16[32]{0:T(256)(128)(2,1)} %param.26) | copy-start | bytes 196
  7.3 42.1 %copy-start.43 = (bf16[32]{0:T(256)(128)(2,1)S(1)}, bf16[32]{0:T(256)(128)(2,1)}, u32[]{:S(2)}) copy-start(bf16[32]{0:T(256)(128)(2,1)} %param.27) | copy-start | bytes 196
  7.3 42.1 %copy-start.44 = (bf16[128]{0:T(256)(128)(2,1)S(1)}, bf16[128]{0:T(256)(128)(2,1)}, u32[]{:S(2)}) copy-start(bf16[128]{0:T(256)(128)(2,1)} %param.29) | copy-start | bytes 772
  7.3 42.1 %copy-start.45 = (bf16[32]{0:T(256)(128)(2,1)S(1)}, bf16[32]{0:T(256)(128)(2,1)}, u32[]{:S(2)}) copy-start(bf16[32]{0:T(256)(128)(2,1)} %param.31) | copy-start | bytes 196
  8.4 16.0 %collective-permute-start = (bf16[128,1024]{1,0:T(8,128)(2,1)S(1)}, bf16[128,1024]{1,0:T(8,128)(2,1)S(1)}, u32[]{:S(2)}, u32[]{:S(2)}) collective-permute-start(bf16[128,1024]{1,0:T(8,128)(2,1)S(1)} %select_bitcast_fusion.3), channel_id=1, source_target_pairs={{0,8},{1,9},{2,10},{3,11},{4,12},{5,13},{6,14},{7,15},{8,0},{9,1},... | collective-permute-start | bytes 786440 | tf_op jit(solution)/shard_map/ppermute | solution.py:276
  25.6 7.6 %collective-permute-start.1 = (bf16[1,128,1024]{2,1,0:T(8,128)(2,1)S(1)}, bf16[1,128,1024]{2,1,0:T(8,128)(2,1)S(1)}, u32[]{:S(2)}, u32[]{:S(2)}) collective-permute-start(bf16[1,128,1024]{2,1,0:T(8,128)(2,1)S(1)} %get-tuple-element.41), channel_id=1, source_target_pairs={{0,2},{1,3},{2,0},{3,1},{4,6},{5,7},{6,4},{7,5},{8,10},{9,11},{10,... | collective-permute-start | bytes 786440 | tf_op jit(solution)/shard_map/ppermute | solution.py:276
  33.3 12.8 %collective-permute-start.2 = (bf16[2,128,1024]{2,1,0:T(8,128)(2,1)S(1)}, bf16[2,128,1024]{2,1,0:T(8,128)(2,1)S(1)}, u32[]{:S(2)}, u32[]{:S(2)}) collective-permute-start(bf16[2,128,1024]{2,1,0:T(8,128)(2,1)S(1)} %pad_maximum_fusion.4), channel_id=1, source_target_pairs={{0,4},{1,5},{2,6},{3,7},{4,0},{5,1},{6,2},{7,3},{8,12},{9,13},{10,... | collective-permute-start | bytes 1572872 | tf_op jit(solution)/shard_map/ppermute | solution.py:276
  47.2 184.1 %copy-start.1 = (bf16[1,128,1024]{2,1,0:T(8,128)(2,1)}, bf16[1,128,1024]{2,1,0:T(8,128)(2,1)S(1)}, u32[]{:S(2)}) copy-start(bf16[1,128,1024]{2,1,0:T(8,128)(2,1)S(1)} %get-tuple-element.39) | copy-start | bytes 786436
  47.2 6.5 %collective-permute-start.3 = (bf16[1,128,1024]{2,1,0:T(8,128)(2,1)S(1)}, bf16[1,128,1024]{2,1,0:T(8,128)(2,1)S(1)}, u32[]{:S(2)}, u32[]{:S(2)}) collective-permute-start(bf16[1,128,1024]{2,1,0:T(8,128)(2,1)S(1)} %get-tuple-element.39), channel_id=1, source_target_pairs={{0,4},{1,5},{2,6},{3,7},{4,0},{5,1},{6,2},{7,3},{8,12},{9,13},{10,... | collective-permute-start | bytes 786440 | tf_op jit(solution)/shard_map/ppermute | solution.py:276
  50.3 9.7 %all-to-all-start = ((bf16[8,33,384]{2,1,0:T(8,128)(2,1)}), bf16[8,33,384]{2,1,0:T(8,128)(2,1)S(1)}, u32[]{:S(2)}, u32[]{:S(2)}) async-start(bf16[8,33,384]{2,1,0:T(8,128)(2,1)} %pad_maximum_fusion.18), calls=%async_computation | async-start | bytes 491520 | tf_op jit(solution)/shard_map/all_to_all | solution.py:376
  53.7 111.8 %all-gather.2.cloned.1.call-start = ((), (), s32[]{:S(2)}) async-start(), calls=%async_computation.7 | async-start | bytes 2162688 | tf_op jit(solution)/shard_map/all_gather | solution.py:432
  53.8 16.9 %collective-permute-start.4 = (bf16[2,128,1024]{2,1,0:T(8,128)(2,1)S(1)}, bf16[2,128,1024]{2,1,0:T(8,128)(2,1)S(1)}, u32[]{:S(2)}, u32[]{:S(2)}) collective-permute-start(bf16[2,128,1024]{2,1,0:T(8,128)(2,1)S(1)} %pad_maximum_fusion.8), channel_id=1, source_target_pairs={{0,2},{1,3},{2,0},{3,1},{4,6},{5,7},{6,4},{7,5},{8,10},{9,11},{10,... | collective-permute-start | bytes 1572872 | tf_op jit(solution)/shard_map/ppermute | solution.py:276
  55.8 84.6 %collective-permute-start.23 = (bf16[128,1024]{1,0:T(8,128)(2,1)S(1)}, bf16[128,1024]{1,0:T(8,128)(2,1)S(1)}, u32[]{:S(2)}, u32[]{:S(2)}) collective-permute-start(bf16[128,1024]{1,0:T(8,128)(2,1)S(1)} %select_bitcast_fusion.1), channel_id=1, source_target_pairs={{0,8},{1,9},{2,10},{3,11},{4,12},{5,13},{6,14},{7,15},{8,0},{9,1},... | collective-permute-start | bytes 786440 | tf_op jit(solution)/shard_map/ppermute | solution.py:276
  59.2 122.1 %collective-permute-start.15 = (bf16[1,128,1024]{2,1,0:T(8,128)(2,1)}, bf16[1,128,1024]{2,1,0:T(8,128)(2,1)}, u32[]{:S(2)}, u32[]{:S(2)}) collective-permute-start(bf16[1,128,1024]{2,1,0:T(8,128)(2,1)} %bitcast.18), channel_id=1, source_target_pairs={{0,8},{1,9},{2,10},{3,11},{4,12},{5,13},{6,14},{7,15},{8,0},{9,1},... | collective-permute-start | bytes 786440 | tf_op jit(solution)/shard_map/ppermute | solution.py:276
  59.9 34.6 %collective-permute-start.6 = (bf16[1,8,33,384]{3,2,1,0:T(8,128)(2,1)S(1)}, bf16[1,8,33,384]{3,2,1,0:T(8,128)(2,1)}, u32[]{:S(2)}, u32[]{:S(2)}) collective-permute-start(bf16[1,8,33,384]{3,2,1,0:T(8,128)(2,1)S(1)} %bitcast.213), channel_id=1, source_target_pairs={{0,8},{1,9},{2,10},{3,11},{4,12},{5,13},{6,14},{7,15},{8,0},{9,1},... | collective-permute-start | bytes 608264 | tf_op jit(solution)/shard_map/ppermute | solution.py:276
  71.8 38.0 %collective-permute-start.5 = (bf16[8,128,1024]{2,1,0:T(8,128)(2,1)}, bf16[8,128,1024]{2,1,0:T(8,128)(2,1)}, u32[]{:S(2)}, u32[]{:S(2)}) collective-permute-start(bf16[8,128,1024]{2,1,0:T(8,128)(2,1)} %get-tuple-element.93), channel_id=1, source_target_pairs={{0,1},{1,0},{2,3},{3,2},{4,5},{5,4},{6,7},{7,6},{8,9},{9,8},{10,11... | collective-permute-start | bytes 6291464 | tf_op jit(solution)/shard_map/ppermute | solution.py:276
  95.6 13.4 %collective-permute-start.7 = (bf16[2,8,33,384]{3,2,1,0:T(8,128)(2,1)S(1)}, bf16[2,8,33,384]{3,2,1,0:T(8,128)(2,1)S(1)}, u32[]{:S(2)}, u32[]{:S(2)}) collective-permute-start(bf16[2,8,33,384]{3,2,1,0:T(8,128)(2,1)S(1)} %pad_maximum_fusion.17), channel_id=1, source_target_pairs={{0,16},{16,0},{1,17},{17,1},{2,18},{18,2},{3,19},{19,3},{4,20},{20... | collective-permute-start | bytes 1216520 | tf_op jit(solution)/shard_map/ppermute | solution.py:276
  136.2 22.5 %all-to-all-start.1 = ((bf16[8,256,128]{2,1,0:T(8,128)(2,1)}), bf16[8,256,128]{2,1,0:T(8,128)(2,1)}, u32[]{:S(2)}, u32[]{:S(2)}) async-start(bf16[8,256,128]{2,1,0:T(8,128)(2,1)} %bitcast.9), calls=%async_computation.1 | async-start | bytes 1048576 | tf_op jit(solution)/shard_map/all_to_all | solution.py:376
  141.4 13.3 %collective-permute-start.24 = (bf16[1,128,1024]{2,1,0:T(8,128)(2,1)S(1)}, bf16[1,128,1024]{2,1,0:T(8,128)(2,1)S(1)}, u32[]{:S(2)}, u32[]{:S(2)}) collective-permute-start(bf16[1,128,1024]{2,1,0:T(8,128)(2,1)S(1)} %get-tuple-element.37), channel_id=1, source_target_pairs={{0,2},{1,3},{2,0},{3,1},{4,6},{5,7},{6,4},{7,5},{8,10},{9,11},{10,... | collective-permute-start | bytes 786440 | tf_op jit(solution)/shard_map/ppermute | solution.py:276
  155.6 16.5 %collective-permute-start.25 = (bf16[2,128,1024]{2,1,0:T(8,128)(2,1)}, bf16[2,128,1024]{2,1,0:T(8,128)(2,1)}, u32[]{:S(2)}, u32[]{:S(2)}) collective-permute-start(bf16[2,128,1024]{2,1,0:T(8,128)(2,1)} %pad_maximum_fusion.6), channel_id=1, source_target_pairs={{0,4},{1,5},{2,6},{3,7},{4,0},{5,1},{6,2},{7,3},{8,12},{9,13},{10,... | collective-permute-start | bytes 1572872 | tf_op jit(solution)/shard_map/ppermute | solution.py:276
  158.8 26.6 %all-to-all-start.2 = ((bf16[8,32,512]{2,1,0:T(8,128)(2,1)}), bf16[8,32,512]{2,1,0:T(8,128)(2,1)}, u32[]{:S(2)}, u32[]{:S(2)}) async-start(bf16[8,32,512]{2,1,0:T(8,128)(2,1)} %reshape.330), calls=%async_computation.2 | async-start | bytes 524288 | tf_op jit(solution)/shard_map/all_to_all | solution.py:376
  168.0 146.4 %copy-start = (f32[2,128,1024]{2,1,0:T(8,128)}, f32[2,128,1024]{2,1,0:T(8,128)S(1)}, u32[]{:S(2)}) copy-start(f32[2,128,1024]{2,1,0:T(8,128)S(1)} %get-tuple-element.129) | copy-start | bytes 3145732
  170.1 8.7 %collective-permute-start.8 = (bf16[1,128,1024]{2,1,0:T(8,128)(2,1)S(1)}, bf16[1,128,1024]{2,1,0:T(8,128)(2,1)S(1)}, u32[]{:S(2)}, u32[]{:S(2)}) collective-permute-start(bf16[1,128,1024]{2,1,0:T(8,128)(2,1)S(1)} %get-tuple-element.90), channel_id=1, source_target_pairs={{0,2},{1,3},{2,0},{3,1},{4,6},{5,7},{6,4},{7,5},{8,10},{9,11},{10,... | collective-permute-start | bytes 786440 | tf_op jit(solution)/shard_map/ppermute | solution.py:276
  175.2 14.2 %collective-permute-start.26 = (bf16[1,128,1024]{2,1,0:T(8,128)(2,1)}, bf16[1,128,1024]{2,1,0:T(8,128)(2,1)}, u32[]{:S(2)}, u32[]{:S(2)}) collective-permute-start(bf16[1,128,1024]{2,1,0:T(8,128)(2,1)} %get-tuple-element.35), channel_id=1, source_target_pairs={{0,4},{1,5},{2,6},{3,7},{4,0},{5,1},{6,2},{7,3},{8,12},{9,13},{10,... | collective-permute-start | bytes 786440 | tf_op jit(solution)/shard_map/ppermute | solution.py:276
  179.6 20.8 %collective-permute-start.9 = (bf16[2,128,1024]{2,1,0:T(8,128)(2,1)}, bf16[2,128,1024]{2,1,0:T(8,128)(2,1)}, u32[]{:S(2)}, u32[]{:S(2)}) collective-permute-start(bf16[2,128,1024]{2,1,0:T(8,128)(2,1)} %pad_maximum_fusion.9), channel_id=1, source_target_pairs={{0,4},{1,5},{2,6},{3,7},{4,0},{5,1},{6,2},{7,3},{8,12},{9,13},{10,... | collective-permute-start | bytes 1572872 | tf_op jit(solution)/shard_map/ppermute | solution.py:276
  183.9 44.7 %collective-permute-start.16 = (bf16[2,128,1024]{2,1,0:T(8,128)(2,1)}, bf16[2,128,1024]{2,1,0:T(8,128)(2,1)}, u32[]{:S(2)}, u32[]{:S(2)}) collective-permute-start(bf16[2,128,1024]{2,1,0:T(8,128)(2,1)} %pad_maximum_fusion.12), channel_id=1, source_target_pairs={{0,16},{16,0},{1,17},{17,1},{2,18},{18,2},{3,19},{19,3},{4,20},{20... | collective-permute-start | bytes 1572872 | tf_op jit(solution)/shard_map/ppermute | solution.py:276
  185.4 38.9 %collective-permute-start.13 = (bf16[1,8,32,512]{3,2,1,0:T(8,128)(2,1)}, bf16[1,8,32,512]{3,2,1,0:T(8,128)(2,1)S(1)}, u32[]{:S(2)}, u32[]{:S(2)}) collective-permute-start(bf16[1,8,32,512]{3,2,1,0:T(8,128)(2,1)} %bitcast.13), channel_id=1, source_target_pairs={{0,8},{1,9},{2,10},{3,11},{4,12},{5,13},{6,14},{7,15},{8,0},{9,1},... | collective-permute-start | bytes 786440 | tf_op jit(solution)/shard_map/ppermute | solution.py:276
  190.5 15.5 %collective-permute-start.27 = (bf16[2,128,1024]{2,1,0:T(8,128)(2,1)S(1)}, bf16[2,128,1024]{2,1,0:T(8,128)(2,1)S(1)}, u32[]{:S(2)}, u32[]{:S(2)}) collective-permute-start(bf16[2,128,1024]{2,1,0:T(8,128)(2,1)S(1)} %pad_maximum_fusion.14), channel_id=1, source_target_pairs={{0,2},{1,3},{2,0},{3,1},{4,6},{5,7},{6,4},{7,5},{8,10},{9,11},{10,... | collective-permute-start | bytes 1572872 | tf_op jit(solution)/shard_map/ppermute | solution.py:276
  204.1 7.2 %collective-permute-start.10 = (bf16[1,128,1024]{2,1,0:T(8,128)(2,1)S(1)}, bf16[1,128,1024]{2,1,0:T(8,128)(2,1)S(1)}, u32[]{:S(2)}, u32[]{:S(2)}) collective-permute-start(bf16[1,128,1024]{2,1,0:T(8,128)(2,1)S(1)} %get-tuple-element.88), channel_id=1, source_target_pairs={{0,4},{1,5},{2,6},{3,7},{4,0},{5,1},{6,2},{7,3},{8,12},{9,13},{10,... | collective-permute-start | bytes 786440 | tf_op jit(solution)/shard_map/ppermute | solution.py:276
  207.1 35.8 %collective-permute-start.28 = (bf16[8,128,1024]{2,1,0:T(8,128)(2,1)}, bf16[8,128,1024]{2,1,0:T(8,128)(2,1)}, u32[]{:S(2)}, u32[]{:S(2)}) collective-permute-start(bf16[8,128,1024]{2,1,0:T(8,128)(2,1)} %get-tuple-element.78), channel_id=1, source_target_pairs={{0,1},{1,0},{2,3},{3,2},{4,5},{5,4},{6,7},{7,6},{8,9},{9,8},{10,11... | collective-permute-start | bytes 6291464 | tf_op jit(solution)/shard_map/ppermute | solution.py:276
  211.4 12.0 %collective-permute-start.11 = (bf16[2,128,1024]{2,1,0:T(8,128)(2,1)S(1)}, bf16[2,128,1024]{2,1,0:T(8,128)(2,1)S(1)}, u32[]{:S(2)}, u32[]{:S(2)}) collective-permute-start(bf16[2,128,1024]{2,1,0:T(8,128)(2,1)S(1)} %pad_maximum_fusion.10), channel_id=1, source_target_pairs={{0,2},{1,3},{2,0},{3,1},{4,6},{5,7},{6,4},{7,5},{8,10},{9,11},{10,... | collective-permute-start | bytes 1572872 | tf_op jit(solution)/shard_map/ppermute | solution.py:276
  224.3 20.4 %collective-permute-start.12 = (bf16[8,128,1024]{2,1,0:T(8,128)(2,1)}, bf16[8,128,1024]{2,1,0:T(8,128)(2,1)}, u32[]{:S(2)}, u32[]{:S(2)}) collective-permute-start(bf16[8,128,1024]{2,1,0:T(8,128)(2,1)} %get-tuple-element.84), channel_id=1, source_target_pairs={{0,1},{1,0},{2,3},{3,2},{4,5},{5,4},{6,7},{7,6},{8,9},{9,8},{10,11... | collective-permute-start | bytes 6291464 | tf_op jit(solution)/shard_map/ppermute | solution.py:276
  227.2 14.3 %collective-permute-start.14 = (bf16[2,8,32,512]{3,2,1,0:T(8,128)(2,1)}, bf16[2,8,32,512]{3,2,1,0:T(8,128)(2,1)}, u32[]{:S(2)}, u32[]{:S(2)}) collective-permute-start(bf16[2,8,32,512]{3,2,1,0:T(8,128)(2,1)} %pad_maximum_fusion.11), channel_id=1, source_target_pairs={{0,16},{16,0},{1,17},{17,1},{2,18},{18,2},{3,19},{19,3},{4,20},{20... | collective-permute-start | bytes 1572872 | tf_op jit(solution)/shard_map/ppermute | solution.py:276
  259.3 13.2 %collective-permute-start.42 = (bf16[2,8,32,512]{3,2,1,0:T(8,128)(2,1)S(1)}, bf16[2,8,32,512]{3,2,1,0:T(8,128)(2,1)S(1)}, u32[]{:S(2)}, u32[]{:S(2)}) collective-permute-start(bf16[2,8,32,512]{3,2,1,0:T(8,128)(2,1)S(1)} %bitcast.217), channel_id=1, source_target_pairs={{0,16},{16,0},{1,17},{17,1},{2,18},{18,2},{3,19},{19,3},{4,20},{20... | collective-permute-start | bytes 1572872 | tf_op jit(solution)/shard_map/ppermute | solution.py:276
  261.0 11.7 %collective-permute-start.17 = (bf16[8,128,1024]{2,1,0:T(8,128)(2,1)S(1)}, bf16[8,128,1024]{2,1,0:T(8,128)(2,1)S(1)}, u32[]{:S(2)}, u32[]{:S(2)}) collective-permute-start(bf16[8,128,1024]{2,1,0:T(8,128)(2,1)S(1)} %slice.400), channel_id=1, source_target_pairs={{0,1},{1,0},{2,3},{3,2},{4,5},{5,4},{6,7},{7,6},{8,9},{9,8},{10,11... | collective-permute-start | bytes 6291464 | tf_op jit(solution)/shard_map/ppermute | solution.py:276
  263.7 11.2 %collective-permute-start.29 = (bf16[8,128,1024]{2,1,0:T(8,128)(2,1)S(1)}, bf16[8,128,1024]{2,1,0:T(8,128)(2,1)S(1)}, u32[]{:S(2)}, u32[]{:S(2)}) collective-permute-start(bf16[8,128,1024]{2,1,0:T(8,128)(2,1)S(1)} %slice.413), channel_id=1, source_target_pairs={{0,1},{1,0},{2,3},{3,2},{4,5},{5,4},{6,7},{7,6},{8,9},{9,8},{10,11... | collective-permute-start | bytes 6291464 | tf_op jit(solution)/shard_map/ppermute | solution.py:276
  269.2 53.7 %collective-permute-start.44 = (bf16[2,128,1024]{2,1,0:T(8,128)(2,1)}, bf16[2,128,1024]{2,1,0:T(8,128)(2,1)}, u32[]{:S(2)}, u32[]{:S(2)}) collective-permute-start(bf16[2,128,1024]{2,1,0:T(8,128)(2,1)} %bitcast.61), channel_id=1, source_target_pairs={{0,16},{16,0},{1,17},{17,1},{2,18},{18,2},{3,19},{19,3},{4,20},{20... | collective-permute-start | bytes 1572872 | tf_op jit(solution)/shard_map/ppermute | solution.py:276
  273.9 17.7 %collective-permute-start.18 = (bf16[2,128,1024]{2,1,0:T(8,128)(2,1)S(1)}, bf16[2,128,1024]{2,1,0:T(8,128)(2,1)S(1)}, u32[]{:S(2)}, u32[]{:S(2)}) collective-permute-start(bf16[2,128,1024]{2,1,0:T(8,128)(2,1)S(1)} %get-tuple-element.61), channel_id=1, source_target_pairs={{0,4},{1,5},{2,6},{3,7},{4,0},{5,1},{6,2},{7,3},{8,12},{9,13},{10,... | collective-permute-start | bytes 1572872 | tf_op jit(solution)/shard_map/ppermute | solution.py:276
  274.6 18.2 %collective-permute-start.20 = (bf16[2,128,1024]{2,1,0:T(8,128)(2,1)S(1)}, bf16[2,128,1024]{2,1,0:T(8,128)(2,1)S(1)}, u32[]{:S(2)}, u32[]{:S(2)}) collective-permute-start(bf16[2,128,1024]{2,1,0:T(8,128)(2,1)S(1)} %get-tuple-element.62), channel_id=1, source_target_pairs={{0,2},{1,3},{2,0},{3,1},{4,6},{5,7},{6,4},{7,5},{8,10},{9,11},{10,... | collective-permute-start | bytes 1572872 | tf_op jit(solution)/shard_map/ppermute | solution.py:276
  276.0 28.2 %collective-permute-start.30 = (bf16[2,128,1024]{2,1,0:T(8,128)(2,1)S(1)}, bf16[2,128,1024]{2,1,0:T(8,128)(2,1)S(1)}, u32[]{:S(2)}, u32[]{:S(2)}) collective-permute-start(bf16[2,128,1024]{2,1,0:T(8,128)(2,1)S(1)} %get-tuple-element.59), channel_id=1, source_target_pairs={{0,4},{1,5},{2,6},{3,7},{4,0},{5,1},{6,2},{7,3},{8,12},{9,13},{10,... | collective-permute-start | bytes 1572872 | tf_op jit(solution)/shard_map/ppermute | solution.py:276
  277.5 26.7 %collective-permute-start.32 = (bf16[2,128,1024]{2,1,0:T(8,128)(2,1)S(1)}, bf16[2,128,1024]{2,1,0:T(8,128)(2,1)S(1)}, u32[]{:S(2)}, u32[]{:S(2)}) collective-permute-start(bf16[2,128,1024]{2,1,0:T(8,128)(2,1)S(1)} %get-tuple-element.60), channel_id=1, source_target_pairs={{0,2},{1,3},{2,0},{3,1},{4,6},{5,7},{6,4},{7,5},{8,10},{9,11},{10,... | collective-permute-start | bytes 1572872 | tf_op jit(solution)/shard_map/ppermute | solution.py:276
  291.6 36.4 %collective-permute-start.43 = (bf16[1,8,32,512]{3,2,1,0:T(8,128)(2,1)}, bf16[1,8,32,512]{3,2,1,0:T(8,128)(2,1)}, u32[]{:S(2)}, u32[]{:S(2)}) collective-permute-start(bf16[1,8,32,512]{3,2,1,0:T(8,128)(2,1)} %broadcast_select_fusion.14), channel_id=1, source_target_pairs={{0,8},{1,9},{2,10},{3,11},{4,12},{5,13},{6,14},{7,15},{8,0},{9,1},... | collective-permute-start | bytes 786440 | tf_op jit(solution)/shard_map/ppermute | solution.py:276
  293.1 11.7 %collective-permute-start.19 = (bf16[1,128,1024]{2,1,0:T(8,128)(2,1)S(1)}, bf16[1,128,1024]{2,1,0:T(8,128)(2,1)S(1)}, u32[]{:S(2)}, u32[]{:S(2)}) collective-permute-start(bf16[1,128,1024]{2,1,0:T(8,128)(2,1)S(1)} %slice.588), channel_id=1, source_target_pairs={{0,2},{1,3},{2,0},{3,1},{4,6},{5,7},{6,4},{7,5},{8,10},{9,11},{10,... | collective-permute-start | bytes 786440 | tf_op jit(solution)/shard_map/ppermute | solution.py:276
  304.2 7.2 %collective-permute-start.21 = (bf16[1,128,1024]{2,1,0:T(8,128)(2,1)S(1)}, bf16[1,128,1024]{2,1,0:T(8,128)(2,1)S(1)}, u32[]{:S(2)}, u32[]{:S(2)}) collective-permute-start(bf16[1,128,1024]{2,1,0:T(8,128)(2,1)S(1)} %slice.587), channel_id=1, source_target_pairs={{0,4},{1,5},{2,6},{3,7},{4,0},{5,1},{6,2},{7,3},{8,12},{9,13},{10,... | collective-permute-start | bytes 786440 | tf_op jit(solution)/shard_map/ppermute | solution.py:276
  304.6 7.0 %collective-permute-start.31 = (bf16[1,128,1024]{2,1,0:T(8,128)(2,1)S(1)}, bf16[1,128,1024]{2,1,0:T(8,128)(2,1)S(1)}, u32[]{:S(2)}, u32[]{:S(2)}) collective-permute-start(bf16[1,128,1024]{2,1,0:T(8,128)(2,1)S(1)} %slice.586), channel_id=1, source_target_pairs={{0,2},{1,3},{2,0},{3,1},{4,6},{5,7},{6,4},{7,5},{8,10},{9,11},{10,... | collective-permute-start | bytes 786440 | tf_op jit(solution)/shard_map/ppermute | solution.py:276
  304.8 9.4 %collective-permute-start.33 = (bf16[1,128,1024]{2,1,0:T(8,128)(2,1)S(1)}, bf16[1,128,1024]{2,1,0:T(8,128)(2,1)S(1)}, u32[]{:S(2)}, u32[]{:S(2)}) collective-permute-start(bf16[1,128,1024]{2,1,0:T(8,128)(2,1)S(1)} %slice.585), channel_id=1, source_target_pairs={{0,4},{1,5},{2,6},{3,7},{4,0},{5,1},{6,2},{7,3},{8,12},{9,13},{10,... | collective-permute-start | bytes 786440 | tf_op jit(solution)/shard_map/ppermute | solution.py:276
  319.4 15.5 %all-to-all-start.3 = ((bf16[8,256,128]{2,1,0:T(8,128)(2,1)}), bf16[8,256,128]{2,1,0:T(8,128)(2,1)S(1)}, u32[]{:S(2)}, u32[]{:S(2)}) async-start(bf16[8,256,128]{2,1,0:T(8,128)(2,1)} %bitcast.203), calls=%async_computation.3 | async-start | bytes 1048576 | tf_op jit(solution)/shard_map/all_to_all | solution.py:376
  325.9 42.8 %collective-permute-start.45 = (bf16[1,128,1024]{2,1,0:T(8,128)(2,1)}, bf16[1,128,1024]{2,1,0:T(8,128)(2,1)}, u32[]{:S(2)}, u32[]{:S(2)}) collective-permute-start(bf16[1,128,1024]{2,1,0:T(8,128)(2,1)} %broadcast_select_fusion.11), channel_id=1, source_target_pairs={{0,8},{1,9},{2,10},{3,11},{4,12},{5,13},{6,14},{7,15},{8,0},{9,1},... | collective-permute-start | bytes 786440 | tf_op jit(solution)/shard_map/ppermute | solution.py:276
  334.9 35.6 %all-to-all-start.5 = ((bf16[8,32,512]{2,1,0:T(8,128)(2,1)}), bf16[8,32,512]{2,1,0:T(8,128)(2,1)}, u32[]{:S(2)}, u32[]{:S(2)}) async-start(bf16[8,32,512]{2,1,0:T(8,128)(2,1)} %fusion.46), calls=%async_computation.6 | async-start | bytes 524288 | tf_op jit(solution)/shard_map/all_to_all | solution.py:376
  339.0 173.8 %reduce-scatter.2.cloned.1.call-start = ((), (), s32[]{:S(2)}) async-start(), calls=%async_computation.8 | async-start | bytes 2162688 | tf_op jit(solution)/shard_map/reduce_scatter | solution.py:518
  365.3 42.9 %collective-permute-start.34 = (bf16[8,128,1024]{2,1,0:T(8,128)(2,1)}, bf16[8,128,1024]{2,1,0:T(8,128)(2,1)}, u32[]{:S(2)}, u32[]{:S(2)}) collective-permute-start(bf16[8,128,1024]{2,1,0:T(8,128)(2,1)} %slice.423), channel_id=1, source_target_pairs={{0,1},{1,0},{2,3},{3,2},{4,5},{5,4},{6,7},{7,6},{8,9},{9,8},{10,11... | collective-permute-start | bytes 6291464 | tf_op jit(solution)/shard_map/ppermute | solution.py:276
  367.2 13.5 %collective-permute-start.40 = (bf16[2,8,33,384]{3,2,1,0:T(8,128)(2,1)}, bf16[2,8,33,384]{3,2,1,0:T(8,128)(2,1)S(1)}, u32[]{:S(2)}, u32[]{:S(2)}) collective-permute-start(bf16[2,8,33,384]{3,2,1,0:T(8,128)(2,1)} %broadcast_select_fusion.8), channel_id=1, source_target_pairs={{0,16},{16,0},{1,17},{17,1},{2,18},{18,2},{3,19},{19,3},{4,20},{20... | collective-permute-start | bytes 1216520 | tf_op jit(solution)/shard_map/ppermute | solution.py:276
  382.1 21.7 %collective-permute-start.41 = (bf16[1,8,33,384]{3,2,1,0:T(8,128)(2,1)S(1)}, bf16[1,8,33,384]{3,2,1,0:T(8,128)(2,1)S(1)}, u32[]{:S(2)}, u32[]{:S(2)}) collective-permute-start(bf16[1,8,33,384]{3,2,1,0:T(8,128)(2,1)S(1)} %broadcast_select_fusion.21), channel_id=1, source_target_pairs={{0,8},{1,9},{2,10},{3,11},{4,12},{5,13},{6,14},{7,15},{8,0},{9,1},... | collective-permute-start | bytes 608264 | tf_op jit(solution)/shard_map/ppermute | solution.py:276
  382.2 35.9 %collective-permute-start.22 = (bf16[128,1024]{1,0:T(8,128)(2,1)S(1)}, bf16[128,1024]{1,0:T(8,128)(2,1)S(1)}, u32[]{:S(2)}, u32[]{:S(2)}) collective-permute-start(bf16[128,1024]{1,0:T(8,128)(2,1)S(1)} %select_bitcast_fusion.2), channel_id=1, source_target_pairs={{0,8},{1,9},{2,10},{3,11},{4,12},{5,13},{6,14},{7,15},{8,0},{9,1},... | collective-permute-start | bytes 786440 | tf_op jit(solution)/shard_map/ppermute | solution.py:276
  404.6 14.4 %all-to-all-start.4 = ((bf16[8,33,384]{2,1,0:T(8,128)(2,1)}), bf16[8,33,384]{2,1,0:T(8,128)(2,1)S(1)}, u32[]{:S(2)}, u32[]{:S(2)}) async-start(bf16[8,33,384]{2,1,0:T(8,128)(2,1)} %fusion.55), calls=%async_computation.4 | async-start | bytes 491520 | tf_op jit(solution)/shard_map/all_to_all | solution.py:376
  414.6 15.5 %collective-permute-start.35 = (bf16[2,128,1024]{2,1,0:T(8,128)(2,1)}, bf16[2,128,1024]{2,1,0:T(8,128)(2,1)}, u32[]{:S(2)}, u32[]{:S(2)}) collective-permute-start(bf16[2,128,1024]{2,1,0:T(8,128)(2,1)} %get-tuple-element.57), channel_id=1, source_target_pairs={{0,4},{1,5},{2,6},{3,7},{4,0},{5,1},{6,2},{7,3},{8,12},{9,13},{10,... | collective-permute-start | bytes 1572872 | tf_op jit(solution)/shard_map/ppermute | solution.py:276
  416.6 16.0 %collective-permute-start.37 = (bf16[2,128,1024]{2,1,0:T(8,128)(2,1)}, bf16[2,128,1024]{2,1,0:T(8,128)(2,1)}, u32[]{:S(2)}, u32[]{:S(2)}) collective-permute-start(bf16[2,128,1024]{2,1,0:T(8,128)(2,1)} %get-tuple-element.58), channel_id=1, source_target_pairs={{0,2},{1,3},{2,0},{3,1},{4,6},{5,7},{6,4},{7,5},{8,10},{9,11},{10,... | collective-permute-start | bytes 1572872 | tf_op jit(solution)/shard_map/ppermute | solution.py:276
  434.9 8.1 %collective-permute-start.36 = (bf16[1,128,1024]{2,1,0:T(8,128)(2,1)S(1)}, bf16[1,128,1024]{2,1,0:T(8,128)(2,1)S(1)}, u32[]{:S(2)}, u32[]{:S(2)}) collective-permute-start(bf16[1,128,1024]{2,1,0:T(8,128)(2,1)S(1)} %slice.584), channel_id=1, source_target_pairs={{0,2},{1,3},{2,0},{3,1},{4,6},{5,7},{6,4},{7,5},{8,10},{9,11},{10,... | collective-permute-start | bytes 786440 | tf_op jit(solution)/shard_map/ppermute | solution.py:276
  437.1 7.4 %collective-permute-start.38 = (bf16[1,128,1024]{2,1,0:T(8,128)(2,1)S(1)}, bf16[1,128,1024]{2,1,0:T(8,128)(2,1)S(1)}, u32[]{:S(2)}, u32[]{:S(2)}) collective-permute-start(bf16[1,128,1024]{2,1,0:T(8,128)(2,1)S(1)} %slice.583), channel_id=1, source_target_pairs={{0,4},{1,5},{2,6},{3,7},{4,0},{5,1},{6,2},{7,3},{8,12},{9,13},{10,... | collective-permute-start | bytes 786440 | tf_op jit(solution)/shard_map/ppermute | solution.py:276
  445.5 14.2 %collective-permute-start.39 = (bf16[128,1024]{1,0:T(8,128)(2,1)S(1)}, bf16[128,1024]{1,0:T(8,128)(2,1)S(1)}, u32[]{:S(2)}, u32[]{:S(2)}) collective-permute-start(bf16[128,1024]{1,0:T(8,128)(2,1)S(1)} %select_bitcast_fusion), channel_id=1, source_target_pairs={{0,8},{1,9},{2,10},{3,11},{4,12},{5,13},{6,14},{7,15},{8,0},{9,1},... | collective-permute-start | bytes 786440 | tf_op jit(solution)/shard_map/ppermute | solution.py:276
  (43 other events, 534.4 us)
Sparse Core Ops, SparseCore 0:
  59.4 73.3 all-gather.1
  375.3 137.3 reduce-scatter.1
